TPU v7x, 32 devices: a whole 2x2x4 slice. The times are simulated.
32 devices in a mesh: dp: 16 (over z, y, x), tensor: 2 (over core).
Axes of the slice: x: 2, y: 2, z: 4, core: 2. Of those that a mesh axis runs over, the one named last changes fastest.
Arguments:
- tokens: bfloat16 [16, 960, 768], P('dp'), may hold values from -6 to 6
- cotangent: bfloat16 [16, 960, 768], P('dp'), may hold values from -24 to 24
- inclusion: int32 [16], P('dp'), may hold values 0 or 1
- attn_weights: float32 [768, 4, 768], P('dp', None, 'tensor'), may hold values from -1.2577882 to 1.2577882
- mlp_weights: float32 [768, 2, 3072], P('dp', None, 'tensor'), may hold values from -0.3247595 to 0.3247595
- attn_momentum: float32 [768, 4, 768], P('dp', None, 'tensor'), may hold values from -6 to 6
- mlp_momentum: float32 [768, 2, 3072], P('dp', None, 'tensor'), may hold values from -20 to 20
- attn_noise: float32 [768, 4, 768], P('dp', None, 'tensor'), may hold values from -6 to 6
- mlp_noise: float32 [768, 2, 3072], P('dp', None, 'tensor'), may hold values from -6 to 6
- vectors: float32 [9216], replicated, may hold values from -0.8 to 1.25
- vector_momentum: float32 [9216], replicated, may hold values from -24 to 24
- vector_noise: float32 [9216], replicated, may hold values from -6 to 6
Outputs:
- out_act: bfloat16 [16, 960, 768], P('dp')
- input_grad: bfloat16 [16, 960, 768], P('dp')
- attn_momentum_new: float32 [768, 4, 768], P('dp', None, 'tensor')
- mlp_momentum_new: float32 [768, 2, 3072], P('dp', None, 'tensor')
- attn_new: float32 [768, 4, 768], P('dp', None, 'tensor')
- mlp_new: float32 [768, 2, 3072], P('dp', None, 'tensor')
- vector_momentum_new: float32 [9216], replicated
- vectors_new: float32 [9216], replicated
All inputs are finite; a program needn't handle non-finite values. No bound on the sum of `inclusion` on one device may be relied on, other than what follows from the above.
Results may differ from a plain program's by a relative error of at most 0.017.
Values may be sent and summed in bfloat16 or wider, within the bound.
A program may use at most 192 MiB of HBM per device.

v0:
```python
import math

import jax
import jax.numpy as jnp
from jax import lax
from jax.sharding import PartitionSpec as P

D = 768
HD = 64
FF = 3072
LEN = 960
NS_ITERS = 5


COEF_A = 3.4445
COEF_B = -4.775
COEF_C = 2.0315


def gelu_tanh(values):
    return jax.nn.gelu(values, approximate=True)


def layer_norm(values, norm_gain, norm_bias):
    centered = values - jnp.mean(values, axis=-1, keepdims=True)
    inverse = lax.rsqrt(jnp.mean(centered * centered, axis=-1, keepdims=True) + 1e-05)
    normed = centered * inverse
    return (normed * norm_gain + norm_bias, normed, inverse)


def norm_back(grad_out, norm_gain, normed, inverse):
    scaled = grad_out * norm_gain
    return inverse * (
        scaled
        - jnp.mean(scaled, axis=-1, keepdims=True)
        - normed * jnp.mean(scaled * normed, axis=-1, keepdims=True)
    )


def contract(left, right, left_dim, right_dim):
    return lax.dot_general(
        left, right, (((left_dim,), (right_dim,)), ((), ())), preferred_element_type=jnp.float32
    )


def causal_mask(length):
    return lax.broadcasted_iota(jnp.int32, (length, length), 0) >= lax.broadcasted_iota(
        jnp.int32, (length, length), 1
    )


def head_forward(head_inputs):
    queries, key_rows, value_rows = head_inputs
    length = queries.shape[0]
    scores = contract(queries, key_rows, 1, 1)
    masked = jnp.where(causal_mask(length), scores, -1e30)
    row_peak = jnp.max(masked, axis=1, keepdims=True)
    logsum = row_peak + jnp.log(jnp.sum(jnp.exp(masked - row_peak), axis=1, keepdims=True))
    probability = jnp.exp(masked - logsum).astype(jnp.bfloat16)
    return (contract(probability, value_rows, 1, 0), logsum[:, 0])


def head_backward(head_inputs):
    queries, key_rows, value_rows, grad_attended, logsum = head_inputs
    length = queries.shape[0]
    scores = contract(queries, key_rows, 1, 1)
    masked = jnp.where(causal_mask(length), scores, -1e30)
    probability = jnp.exp(masked - logsum[:, None])
    prob_low = probability.astype(jnp.bfloat16)
    grad_prob = contract(grad_attended, value_rows, 1, 1)
    grad_value = contract(prob_low, grad_attended, 0, 0)
    inner = jnp.sum(probability * grad_prob, axis=1, keepdims=True)
    grad_scores = (probability * (grad_prob - inner)).astype(jnp.bfloat16)
    grad_query = contract(grad_scores, key_rows, 1, 0)
    grad_key = contract(grad_scores, queries, 0, 0)
    query_scale = 1.0 / math.sqrt(HD)
    return (
        (grad_query * query_scale).astype(jnp.bfloat16),
        grad_key.astype(jnp.bfloat16),
        grad_value.astype(jnp.bfloat16),
    )


def newton(owned_columns, tensor_index):
    column_count = owned_columns.shape[1]
    matrix = lax.all_gather(
        owned_columns.astype(jnp.bfloat16), "tensor", axis=1, tiled=True
    ).astype(owned_columns.dtype)
    current = matrix / (jnp.sqrt(jnp.sum(matrix * matrix)) + 1e-07)
    for iteration in range(NS_ITERS):
        gram_matrix = lax.dot_general(
            current, current, (((1,), (1,)), ((), ())), precision=lax.Precision.HIGHEST
        )
        polynomial = COEF_B * gram_matrix + COEF_C * jnp.dot(
            gram_matrix, gram_matrix, precision=lax.Precision.HIGHEST
        )
        current = COEF_A * current + jnp.dot(polynomial, current, precision=lax.Precision.HIGHEST)
    return lax.dynamic_slice_in_dim(current, tensor_index * column_count, column_count, 1)


def placed(piece, start, total_size):
    return lax.dynamic_update_slice_in_dim(jnp.zeros((total_size,), jnp.float32), piece, start, 0)


def body(
    tokens,
    cotangent,
    inclusion,
    attn_weights,
    mlp_weights,
    attn_momentum,
    mlp_momentum,
    attn_noise,
    mlp_noise,
    vectors,
    vector_momentum,
    vector_noise,
):
    dp_count = lax.axis_size("dp")
    dp_index = lax.axis_index("dp")
    halves = lax.axis_size("tensor")
    tensor_index = lax.axis_index("tensor")
    head_width = D // halves
    hidden_width = FF // halves
    local_heads = head_width // HD
    query_scale = 1.0 / math.sqrt(HD)
    clip = 1.5 * D * math.sqrt(LEN)
    sigma = 0.05 * math.sqrt(dp_count) / D
    batch = 0.75 * dp_count
    attn_low, mlp_low = (
        lax.all_gather(attn_weights.astype(jnp.bfloat16), "dp", axis=0, tiled=True),
        lax.all_gather(mlp_weights.astype(jnp.bfloat16), "dp", axis=0, tiled=True),
    )
    gain_one = vectors[0:D]
    bias_one = vectors[D : 2 * D]
    gain_two = vectors[2 * D : 3 * D]
    bias_two = vectors[3 * D : 4 * D]
    query_bias = lax.dynamic_slice_in_dim(vectors, 4 * D + tensor_index * head_width, head_width)
    value_bias = lax.dynamic_slice_in_dim(vectors, 5 * D + tensor_index * head_width, head_width)
    attn_bias = vectors[6 * D : 7 * D]
    mlp_bias = vectors[7 * D : 8 * D]
    hidden_bias = lax.dynamic_slice_in_dim(
        vectors, 8 * D + tensor_index * hidden_width, hidden_width
    )
    inputs = tokens[0].astype(jnp.float32)
    length = inputs.shape[0]
    share_rows = length // halves
    share_start = tensor_index * share_rows
    first, normed_one, inverse_one = layer_norm(inputs, gain_one, bias_one)
    first_low = first.astype(jnp.bfloat16)
    in_weights = attn_low[:, 0:3, :]
    projected = jnp.einsum("ld,djh->ljh", first_low, in_weights, preferred_element_type=jnp.float32)
    queries = ((projected[:, 0, :] + query_bias) * query_scale).astype(jnp.bfloat16)
    key_rows = projected[:, 1, :].astype(jnp.bfloat16)
    value_rows = (projected[:, 2, :] + value_bias).astype(jnp.bfloat16)

    def to_heads(matrix):
        return matrix.reshape(length, local_heads, HD).transpose(1, 0, 2)

    def from_heads(stacked):
        return stacked.transpose(1, 0, 2).reshape(length, head_width)

    head_queries = to_heads(queries)
    head_keys = to_heads(key_rows)
    head_values = to_heads(value_rows)
    attended, logsums = lax.map(head_forward, (head_queries, head_keys, head_values))
    attended_low = from_heads(attended).astype(jnp.bfloat16)
    out_weight = attn_low[:, 3, :]
    attn_total = lax.psum(
        contract(attended_low, out_weight, 1, 1).astype(jnp.bfloat16), "tensor"
    ).astype(jnp.float32)
    middle = inputs + attn_total + attn_bias
    second, normed_two, inverse_two = layer_norm(middle, gain_two, bias_two)
    second_low = second.astype(jnp.bfloat16)
    fc_weight = mlp_low[:, 0, :]
    pr_weight = mlp_low[:, 1, :]
    pre_act = contract(second_low, fc_weight, 1, 0) + hidden_bias
    activation, gelu_back = jax.vjp(gelu_tanh, pre_act)
    activation_low = activation.astype(jnp.bfloat16)
    mlp_total = lax.psum(
        contract(activation_low, pr_weight, 1, 1).astype(jnp.bfloat16), "tensor"
    ).astype(jnp.float32)
    result = middle + mlp_total + mlp_bias
    cot_low = cotangent[0]
    grad_out = cot_low.astype(jnp.float32)
    d_pr = contract(cot_low, activation_low, 0, 0)
    grad_pre = gelu_back(contract(cot_low, pr_weight, 1, 0))[0].astype(jnp.bfloat16)
    d_fc = contract(second_low, grad_pre, 0, 0)
    d_hidden_bias = jnp.sum(grad_pre.astype(jnp.float32), axis=0)
    grad_two = lax.psum_scatter(
        contract(grad_pre, fc_weight, 1, 1).astype(jnp.bfloat16),
        "tensor",
        scatter_dimension=0,
        tiled=True,
    ).astype(jnp.float32)
    normed_two_share = lax.dynamic_slice_in_dim(normed_two, share_start, share_rows, 0)
    inverse_two_share = lax.dynamic_slice_in_dim(inverse_two, share_start, share_rows, 0)
    grad_out_share = lax.dynamic_slice_in_dim(grad_out, share_start, share_rows, 0)
    grad_mid = grad_out_share + norm_back(grad_two, gain_two, normed_two_share, inverse_two_share)
    gain_two_part = jnp.sum(grad_two * normed_two_share, axis=0)
    bias_two_part = jnp.sum(grad_two, axis=0)
    attn_bias_part = jnp.sum(grad_mid, axis=0)
    d_gain_two, d_bias_two, d_attn_bias = lax.psum(
        (gain_two_part, bias_two_part, attn_bias_part), "tensor"
    )
    d_mlp_bias = jnp.sum(grad_out, axis=0)
    mid_low = lax.all_gather(grad_mid.astype(jnp.bfloat16), "tensor", axis=0, tiled=True)
    d_out = contract(mid_low, attended_low, 0, 0)
    grad_attended = contract(mid_low, out_weight, 1, 0).astype(jnp.bfloat16)
    grad_q, grad_k, grad_v = lax.map(
        head_backward, (head_queries, head_keys, head_values, to_heads(grad_attended), logsums)
    )
    grad_proj = jnp.stack([from_heads(grad_q), from_heads(grad_k), from_heads(grad_v)], axis=1)
    d_proj = jnp.einsum("ld,ljh->djh", first_low, grad_proj, preferred_element_type=jnp.float32)
    proj_bias_grads = jnp.sum(grad_proj.astype(jnp.float32), axis=0)
    back_one = jnp.einsum("ljh,djh->ld", grad_proj, in_weights, preferred_element_type=jnp.float32)
    split_square = (
        jnp.sum(d_proj * d_proj)
        + jnp.sum(d_out * d_out)
        + jnp.sum(d_fc * d_fc)
        + jnp.sum(d_pr * d_pr)
        + jnp.sum(proj_bias_grads[0] * proj_bias_grads[0])
        + jnp.sum(proj_bias_grads[2] * proj_bias_grads[2])
        + jnp.sum(d_hidden_bias * d_hidden_bias)
    )
    grad_one = lax.psum_scatter(
        back_one.astype(jnp.bfloat16), "tensor", scatter_dimension=0, tiled=True
    ).astype(jnp.float32)
    normed_one_share = lax.dynamic_slice_in_dim(normed_one, share_start, share_rows, 0)
    inverse_one_share = lax.dynamic_slice_in_dim(inverse_one, share_start, share_rows, 0)
    grad_in = grad_mid + norm_back(grad_one, gain_one, normed_one_share, inverse_one_share)
    gain_one_part = jnp.sum(grad_one * normed_one_share, axis=0)
    bias_one_part = jnp.sum(grad_one, axis=0)
    split_total, d_gain_one, d_bias_one = lax.psum(
        (split_square, gain_one_part, bias_one_part), "tensor"
    )
    input_full = lax.all_gather(grad_in.astype(jnp.bfloat16), "tensor", axis=0, tiled=True)
    shared_square = (
        jnp.sum(d_gain_one * d_gain_one)
        + jnp.sum(d_bias_one * d_bias_one)
        + jnp.sum(d_gain_two * d_gain_two)
        + jnp.sum(d_bias_two * d_bias_two)
        + jnp.sum(d_attn_bias * d_attn_bias)
        + jnp.sum(d_mlp_bias * d_mlp_bias)
    )
    total_square = split_total + shared_square
    factor = inclusion[0].astype(jnp.float32) * jnp.minimum(
        1.0, clip / (jnp.sqrt(total_square) + 1e-06)
    )
    attn_grad = jnp.concatenate([d_proj, d_out[:, None, :]], axis=1) * factor
    mlp_grad = jnp.stack([d_fc, d_pr], axis=1) * factor
    attn_summed, mlp_summed = (
        lax.psum_scatter(attn_grad, "dp", scatter_dimension=0, tiled=True),
        lax.psum_scatter(mlp_grad, "dp", scatter_dimension=0, tiled=True),
    )
    leading = (tensor_index == 0).astype(jnp.float32)
    vector_grad = (
        jnp.concatenate(
            [
                leading * d_gain_one,
                leading * d_bias_one,
                leading * d_gain_two,
                leading * d_bias_two,
                placed(proj_bias_grads[0], tensor_index * head_width, D),
                placed(proj_bias_grads[2], tensor_index * head_width, D),
                leading * d_attn_bias,
                leading * d_mlp_bias,
                placed(d_hidden_bias, tensor_index * hidden_width, FF),
            ]
        )
        * factor
    )
    vector_summed = lax.psum(vector_grad, ("dp", "tensor"))
    noise_scale = sigma * clip
    attn_moment = 0.5 * attn_momentum + (attn_summed + noise_scale * attn_noise) / batch
    mlp_moment = 0.5 * mlp_momentum + (mlp_summed + noise_scale * mlp_noise) / batch
    vector_moment = 0.5 * vector_momentum + (vector_summed + noise_scale * vector_noise) / batch
    vector_rate = 0.2 * math.sqrt(dp_count / LEN)
    vectors_new = vectors - vector_rate * vector_moment
    owner_list = [slot_index * dp_count // 6 for slot_index in range(6)]
    full_attn, full_mlp = (
        lax.all_gather(attn_moment.astype(jnp.bfloat16), "dp", axis=0, tiled=True).astype(
            attn_moment.dtype
        ),
        lax.all_gather(mlp_moment.astype(jnp.bfloat16), "dp", axis=0, tiled=True).astype(
            mlp_moment.dtype
        ),
    )
    attn_pick = jnp.array(owner_list[0:4]) == dp_index
    mlp_pick = jnp.array(owner_list[4:6]) == dp_index
    mine_attn = jnp.sum(jnp.where(attn_pick[None, :, None], full_attn, 0.0), axis=1)
    mine_mlp = jnp.sum(jnp.where(mlp_pick[None, :, None], full_mlp, 0.0), axis=1)
    orthogonal = newton(
        jnp.pad(mine_attn, ((0, 0), (0, hidden_width - head_width))) + mine_mlp, tensor_index
    )
    attn_back_rows = jnp.where(attn_pick[None, :, None], orthogonal[:, None, 0:head_width], 0.0)
    mlp_back_rows = jnp.where(mlp_pick[None, :, None], orthogonal[:, None, :], 0.0)
    attn_orth, mlp_orth = (
        lax.psum_scatter(attn_back_rows, "dp", scatter_dimension=0, tiled=True),
        lax.psum_scatter(mlp_back_rows, "dp", scatter_dimension=0, tiled=True),
    )
    attn_rates = jnp.array([0.5, 0.5, 0.5, 0.5 * max(1.0, math.sqrt(LEN) / 8.0)], jnp.float32)
    mlp_rates = jnp.array([0.5 * math.sqrt(FF / D), 0.5], jnp.float32)
    attn_new = attn_weights - attn_rates[None, :, None] * attn_orth
    mlp_new = mlp_weights - mlp_rates[None, :, None] * mlp_orth
    return (
        result.astype(jnp.bfloat16)[None],
        input_full[None],
        attn_moment,
        mlp_moment,
        attn_new,
        mlp_new,
        vector_moment,
        vectors_new,
    )


def solution(mesh):
    in_specs = (
        P("dp", None, None),
        P("dp", None, None),
        P("dp"),
        P("dp", None, "tensor"),
        P("dp", None, "tensor"),
        P("dp", None, "tensor"),
        P("dp", None, "tensor"),
        P("dp", None, "tensor"),
        P("dp", None, "tensor"),
        P(),
        P(),
        P(),
    )
    out_specs = (
        P("dp", None, None),
        P("dp", None, None),
        P("dp", None, "tensor"),
        P("dp", None, "tensor"),
        P("dp", None, "tensor"),
        P("dp", None, "tensor"),
        P(),
        P(),
    )
    return jax.shard_map(body, mesh=mesh, in_specs=in_specs, out_specs=out_specs, check_vma=False)
```

profile of v0, /device:TPU:30, one launch (start us, length us, event | category | flops | bytes accessed | tf_op | source)
XLA Modules:
  0.0 1509.6 jit_solution(14168591962262331724)
XLA Ops:
  13.0 59.5 %all-gather.8.cloned.1.call-done = bf16[768,4,384]{2,0,1:T(8,128)(2,1)} async-done(((bf16[48,4,384]{2,0,1:T(8,128)(2,1)}), bf16[768,4,384]{2,0,1:T(8,128)(2,1)}) %all-gather.8.cloned.1.call-update) | async-done | bytes 2359312 | tf_op jit(solution)/shard_map/all_gather | solution.py:131
  72.5 3.8 fusion.99
  82.2 2.4 copy.49
  86.4 3.0 copy.44
  89.4 2.5 fusion.127
  91.9 2.4 copy.47
  94.3 34.1 %while.26 = (s32[]{:T(128)}, bf16[6,960,64]{1,2,0:T(8,128)(2,1)}, f32[6,960]{1,0:T(8,128)}, bf16[6,960,64]{2,1,0:T(8,128)(2,1)}, bf16[6,960,64]{2,1,0:T(8,128)(2...) while((s32[]{:T(128)}, bf16[6,960,64]{1,2,0:T(8,128)(2,1)}, f32[6,960]{1,0:T(8,128)}, ...), condition=%wide.region_5.6_spmd, body=%wide.region_2.5_spmd.sunk | while | flops 246066240 | bytes 12095329 | solution.py:166
  128.4 3.4 convolution_convert_fusion.1
  133.8 19.7 %all-reduce.5.cloned.1.call-done = bf16[960,768]{1,0:T(8,128)(2,1)} async-done(((bf16[960,768]{1,0:T(8,128)(2,1)}), bf16[960,768]{1,0:T(8,128)(2,1)}) %all-reduce.5.cloned.1.call-update) | async-done | bytes 1474576 | tf_op jit(solution)/shard_map/psum | solution.py:169
  155.5 2.9 fusion.65
  160.6 75.2 %all-gather.10.cloned.1.call-done = bf16[768,2,1536]{2,0,1:T(8,128)(2,1)} async-done(((bf16[48,2,1536]{2,0,1:T(8,128)(2,1)}), bf16[768,2,1536]{2,0,1:T(8,128)(2,1)}) %all-gather.10.cloned.1.call-update) | async-done | bytes 4718608 | tf_op jit(solution)/shard_map/all_gather | solution.py:132
  235.9 5.1 fusion.86
  241.0 6.3 convert_reduce_fusion
  249.0 3.6 fusion.97
  252.6 3.2 bitcast_convert_fusion.1
  255.9 7.0 reduce-scatter.7.cloned.1.call-done
  265.1 2.5 fusion.156
  273.1 7.5 all-gather.12.cloned.1.call-done
  280.7 3.3 convolution_convert_fusion.2
  286.2 67.3 %while.27 = (s32[]{:T(128)}, bf16[6,960,64]{1,2,0:T(8,128)(2,1)}, bf16[6,960,64]{1,2,0:T(8,128)(2,1)}, bf16[6,960,64]{1,2,0:T(8,128)(2,1)}, bf16[6,960,64]{2,1,0...) while((s32[]{:T(128)}, bf16[6,960,64]{1,2,0:T(8,128)(2,1)}, ...), condition=%wide.region_15.16_spmd, body=%wide.region_13.15_spmd.sunk | while | flops 598363200 | bytes 29925488 | solution.py:210
  293.9 2.3 fusion.228
  305.1 2.3 fusion.228
  325.3 2.3 fusion.229
  336.5 2.3 fusion.229
  356.8 2.6 copy.57
  359.4 4.9 bitcast_convert_fusion
  364.6 8.3 multiply_reduce_fusion.1
  372.9 9.2 fusion.60
  382.9 3.4 multiply_reduce_fusion.4
  386.4 4.9 multiply_reduce_fusion.2
  399.2 4.0 all-reduce.1
  411.6 4.4 maximum_multiply_fusion.1
  416.1 8.5 maximum_multiply_fusion
  424.7 127.9 %reduce-scatter.11.cloned.1.call-done = f32[48,4,384]{2,0,1:T(8,128)} async-done(((f32[768,4,384]{2,0,1:T(8,128)}), f32[48,4,384]{2,0,1:T(8,128)}) %reduce-scatter.11.cloned.1.call-update) | async-done | bytes 294928 | tf_op jit(solution)/shard_map/reduce_scatter | solution.py:253
  554.4 173.9 %reduce-scatter.13.cloned.1.call-done = f32[48,2,1536]{2,0,1:T(8,128)} async-done(((f32[768,2,1536]{2,0,1:T(8,128)}), f32[48,2,1536]{2,0,1:T(8,128)}) %reduce-scatter.13.cloned.1.call-update) | async-done | bytes 589840 | tf_op jit(solution)/shard_map/reduce_scatter | solution.py:254
  730.5 62.2 %all-gather.16.cloned.1.call-done = bf16[768,4,384]{2,0,1:T(8,128)(2,1)} async-done(((bf16[48,4,384]{2,0,1:T(8,128)(2,1)}), bf16[768,4,384]{2,0,1:T(8,128)(2,1)}) %all-gather.16.cloned.1.call-update) | async-done | bytes 2359312 | tf_op jit(solution)/shard_map/all_gather | solution.py:282
  792.8 2.3 select_reduce_fusion.1
  795.1 79.9 %all-gather.18.cloned.1.call-done = bf16[768,2,1536]{2,0,1:T(8,128)(2,1)} async-done(((bf16[48,2,1536]{2,0,1:T(8,128)(2,1)}), bf16[768,2,1536]{2,0,1:T(8,128)(2,1)}) %all-gather.18.cloned.1.call-update) | async-done | bytes 4718608 | tf_op jit(solution)/shard_map/all_gather | solution.py:285
  875.0 4.1 select_reduce_fusion
  881.1 8.4 fusion.96
  889.7 2.9 fusion.104
  892.6 4.2 all-gather.20.cloned.1.call-done
  896.8 5.4 fusion.51
  903.0 26.6 %fusion.59 = f32[768,768]{1,0:T(8,128)S(1)} fusion(bf16[768,3072]{1,0:T(8,128)(2,1)} %all-gather.20.cloned.1.call-done, f32[]{:T(128)S(6)} %add.336), kind=kOutput, calls=%fused_computation.76 | convolution fusion | flops 21747990528 | bytes 7077892 | tf_op jit(solution)/shard_map/dot_general | solution.py:91
  929.6 6.0 fusion.161
  935.6 24.4 %multiply_add_fusion.3 = f32[768,3072]{1,0:T(8,128)S(1)} fusion(bf16[768,3072]{1,0:T(8,128)(2,1)S(1)} %bitcast.233, f32[]{:T(128)S(6)} %add.336, f32[768,768]{1,0:T(8,128)S(1)} %fusion.161, f32[768,768]{1,0:T(8,128)S(1)} %fusion.59), kind=kOutput, calls=%fused_computation.63 | convolution fusion | flops 21759197184 | bytes 18874372 | tf_op jit(solution)/shard_map/dot_general | solution.py:97
  960.0 23.9 %fusion.162 = f32[768,768]{1,0:T(8,128)S(1)} fusion(f32[768,3072]{1,0:T(8,128)S(1)} %multiply_add_fusion.3), kind=kOutput, calls=%fused_computation.249 | convolution fusion | flops 21743271936 | bytes 11796480 | tf_op jit(solution)/shard_map/dot_general | solution.py:91
  983.9 6.0 fusion.163
  989.9 24.5 %multiply_add_fusion.2 = f32[768,3072]{1,0:T(8,128)S(1)} fusion(f32[768,3072]{1,0:T(8,128)S(1)} %multiply_add_fusion.3, f32[768,768]{1,0:T(8,128)S(1)} %fusion.163, f32[768,768]{1,0:T(8,128)S(1)} %fusion.162), kind=kOutput, calls=%fused_computation.62 | convolution fusion | flops 21749760000 | bytes 23592960 | tf_op jit(solution)/shard_map/dot_general | solution.py:97
  1014.4 23.9 %fusion.164 = f32[768,768]{1,0:T(8,128)S(1)} fusion(f32[768,3072]{1,0:T(8,128)S(1)} %multiply_add_fusion.2), kind=kOutput, calls=%fused_computation.251 | convolution fusion | flops 21743271936 | bytes 11796480 | tf_op jit(solution)/shard_map/dot_general | solution.py:91
  1038.2 6.0 fusion.165
  1044.2 24.5 %multiply_add_fusion.1 = f32[768,3072]{1,0:T(8,128)S(1)} fusion(f32[768,3072]{1,0:T(8,128)S(1)} %multiply_add_fusion.2, f32[768,768]{1,0:T(8,128)S(1)} %fusion.165, f32[768,768]{1,0:T(8,128)S(1)} %fusion.164), kind=kOutput, calls=%fused_computation.61 | convolution fusion | flops 21749760000 | bytes 23592960 | tf_op jit(solution)/shard_map/dot_general | solution.py:97
  1068.7 23.9 %fusion.166 = f32[768,768]{1,0:T(8,128)S(1)} fusion(f32[768,3072]{1,0:T(8,128)S(1)} %multiply_add_fusion.1), kind=kOutput, calls=%fused_computation.253 | convolution fusion | flops 21743271936 | bytes 11796480 | tf_op jit(solution)/shard_map/dot_general | solution.py:91
  1092.6 6.0 fusion.167
  1098.6 27.1 %multiply_add_fusion = f32[768,3072]{1,0:T(8,128)S(1)} fusion(f32[768,3072]{1,0:T(8,128)} %copy-done.43, f32[768,768]{1,0:T(8,128)S(1)} %fusion.167, f32[768,768]{1,0:T(8,128)S(1)} %fusion.166), kind=kOutput, calls=%fused_computation.60 | convolution fusion | flops 21749760000 | bytes 23592960 | tf_op jit(solution)/shard_map/dot_general | solution.py:97
  1125.7 24.3 %fusion.168 = f32[768,768]{1,0:T(8,128)S(1)} fusion(f32[768,3072]{1,0:T(8,128)S(1)} %multiply_add_fusion), kind=kOutput, calls=%fused_computation.255 | convolution fusion | flops 21743271936 | bytes 11796480 | tf_op jit(solution)/shard_map/dot_general | solution.py:91
  1150.1 6.0 fusion.169
  1156.0 23.7 %fusion.69 = f32[768,3072]{1,0:T(8,128)S(1)} fusion(f32[768,3072]{1,0:T(8,128)S(1)} %multiply_add_fusion, f32[768,768]{1,0:T(8,128)S(1)} %fusion.169, f32[768,768]{1,0:T(8,128)S(1)} %fusion.168), kind=kOutput, calls=%fused_computation.107 | convolution fusion | flops 21745041408 | bytes 23592960 | tf_op jit(solution)/shard_map/dot_general | solution.py:97
  1183.3 2.6 broadcast_select_fusion.1
  1185.9 7.3 broadcast_select_fusion
  1195.1 3.2 fusion.113
  1198.4 40.1 %psum.71 = f32[9216]{0:T(1024)S(1)} all-reduce(f32[9216]{0:T(1024)S(1)} %broadcast_multiply_fusion), channel_id=1, replica_groups=mesh['dp'=16,'tensor'=2] {'dp','tensor'}, use_global_device_ids=true, to_apply=%region_53.54 | all-reduce | flops 9216 | bytes 73728 | tf_op jit(solution)/shard_map/psum | solution.py:273
  1243.0 80.4 %reduce-scatter.15.cloned.1.call-done = f32[48,4,384]{2,0,1:T(8,128)} async-done(((f32[768,4,384]{2,0,1:T(8,128)}), f32[48,4,384]{2,0,1:T(8,128)}) %reduce-scatter.15.cloned.1.call-update) | async-done | bytes 294928 | tf_op jit(solution)/shard_map/reduce_scatter | solution.py:299
  1325.3 173.9 %reduce-scatter.17.cloned.1.call-done = f32[48,2,1536]{2,0,1:T(8,128)} async-done(((f32[768,2,1536]{2,0,1:T(8,128)}), f32[48,2,1536]{2,0,1:T(8,128)}) %reduce-scatter.17.cloned.1.call-update) | async-done | bytes 589840 | tf_op jit(solution)/shard_map/reduce_scatter | solution.py:300
  (273 shorter events, 155.7 us)
Async XLA Ops:
  7.2 5.2 copy-start.25
  7.2 4.6 copy-start
  7.2 65.3 %all-gather.8.cloned.1.call-start = ((), (), s32[]{:S(2)}) async-start(), calls=%async_computation.6 | async-start | bytes 2506752 | tf_op jit(solution)/shard_map/all_gather | solution.py:131
  9.0 144.5 %all-reduce.5.cloned.1.call-start = ((), (), s32[]{:S(2)}) async-start(), calls=%async_computation.7 | async-start | bytes 2949120 | tf_op jit(solution)/shard_map/psum | solution.py:169
  12.4 60.1 %copy-start.31 = (f32[960]{0:T(1024)}, f32[960]{0:T(1024)S(1)}, u32[]{:S(2)}) copy-start(f32[960]{0:T(1024)S(1)} %add_rsqrt_fusion.1) | copy-start | bytes 11524
  13.0 63.3 %copy-start.36 = (f32[768]{0:T(1024)}, f32[768]{0:T(1024)S(1)}, u32[]{:S(2)}) copy-start(f32[768]{0:T(1024)S(1)} %get-tuple-element.192) | copy-start | bytes 9220
  13.0 145.4 %copy-start.26 = (f32[768]{0:T(1024)}, f32[768]{0:T(1024)S(1)}, u32[]{:S(2)}) copy-start(f32[768]{0:T(1024)S(1)} %get-tuple-element.191) | copy-start | bytes 9220
  128.4 3.5 copy-start.18
  131.9 104.0 %all-gather.10.cloned.1.call-start = ((), (), s32[]{:S(2)}) async-start(), calls=%async_computation.8 | async-start | bytes 5013504 | tf_op jit(solution)/shard_map/all_gather | solution.py:132
  132.7 22.8 %copy-start.32 = (f32[960]{0:T(1024)S(1)}, f32[960]{0:T(1024)}, u32[]{:S(2)}) copy-start(f32[960]{0:T(1024)} %copy-done.31) | copy-start | bytes 11524
  132.7 130.2 %reduce-scatter.7.cloned.1.call-start = ((), (), s32[]{:S(2)}) async-start(), calls=%async_computation.10 | async-start | bytes 2211840 | tf_op jit(solution)/shard_map/reduce_scatter | solution.py:190
  133.8 239.1 %copy-start.34 = (f32[1536]{0:T(1024)}, f32[1536]{0:T(1024)S(1)}, u32[]{:S(2)}) copy-start(f32[1536]{0:T(1024)S(1)} %dynamic_slice.51) | copy-start | bytes 18436
  153.5 2.1 copy-start.3
  158.4 77.4 %copy-start.38 = (f32[768]{0:T(1024)S(1)}, f32[768]{0:T(1024)}, u32[]{:S(2)}) copy-start(f32[768]{0:T(1024)} %get-tuple-element.189) | copy-start | bytes 9220
  235.9 5.2 copy-start.7
  235.9 5.2 copy-start.40
  241.0 6.3 copy-start.44
  247.3 1.6 copy-start.45
  247.3 25.1 %copy-start.30 = (f32[1536]{0:T(1024)}, f32[1536]{0:T(1024)S(1)}, u32[]{:S(2)}) copy-start(f32[1536]{0:T(1024)S(1)} %get-tuple-element.216) | copy-start | bytes 18436
  252.6 28.1 %all-gather.12.cloned.1.call-start = ((), (), s32[]{:S(2)}) async-start(), calls=%async_computation.11 | async-start | bytes 2211840 | tf_op jit(solution)/shard_map/all_gather | solution.py:207
  267.6 1.1 copy-start.5
  269.7 127.4 %reduce-scatter.9.cloned.1.call-start = ((), (), s32[]{:S(2)}) async-start(), calls=%async_computation.12 | async-start | bytes 2211840 | tf_op jit(solution)/shard_map/reduce_scatter | solution.py:226
  355.0 9.4 copy-start.10
  356.7 7.6 copy-start.13
  364.4 8.5 copy-start.8
  364.4 188.2 %reduce-scatter.11.cloned.1.call-start = ((), (), s32[]{:S(2)}) async-start(), calls=%async_computation.14 | async-start | bytes 5013504 | tf_op jit(solution)/shard_map/reduce_scatter | solution.py:253
  372.9 9.2 copy-start.11
  372.9 9.2 copy-start.14
  372.9 9.2 copy-start.16
  382.9 3.5 copy-start.12
  382.9 3.5 copy-start.15
  382.9 3.5 copy-start.17
  382.9 3.5 copy-start.37
  410.2 5.9 copy-start.28
  416.1 312.2 %reduce-scatter.13.cloned.1.call-start = ((), (), s32[]{:S(2)}) async-start(), calls=%async_computation.15 | async-start | bytes 10027008 | tf_op jit(solution)/shard_map/reduce_scatter | solution.py:254
  424.6 128.0 %copy-start.23 = (f32[48,4,384]{2,1,0:T(4,128)S(1)}, f32[48,4,384]{2,1,0:T(4,128)}, u32[]{:S(2)}) copy-start(f32[48,4,384]{2,1,0:T(4,128)} %param.27) | copy-start | bytes 884740
  424.6 128.0 %copy-start.24 = (f32[48,4,384]{2,1,0:T(4,128)S(1)}, f32[48,4,384]{2,1,0:T(4,128)}, u32[]{:S(2)}) copy-start(f32[48,4,384]{2,1,0:T(4,128)} %param.25) | copy-start | bytes 884740
  424.6 303.7 %copy-start.21 = (f32[48,2,1536]{2,1,0:T(2,128)S(1)}, f32[48,2,1536]{2,1,0:T(2,128)}, u32[]{:S(2)}) copy-start(f32[48,2,1536]{2,1,0:T(2,128)} %param.28) | copy-start | bytes 1769476
  424.6 303.7 %copy-start.22 = (f32[48,2,1536]{2,1,0:T(2,128)S(1)}, f32[48,2,1536]{2,1,0:T(2,128)}, u32[]{:S(2)}) copy-start(f32[48,2,1536]{2,1,0:T(2,128)} %param.26) | copy-start | bytes 1769476
  424.6 305.9 %copy-start.42 = (s32[4]{0:T(128)S(1)}, s32[4]{0:T(128)}, u32[]{:S(2)}) copy-start(s32[4]{0:T(128)} %constant.146.clone) | copy-start | bytes 52
  424.6 305.9 %copy-start.41 = (s32[2]{0:T(128)S(1)}, s32[2]{0:T(128)}, u32[]{:S(2)}) copy-start(s32[2]{0:T(128)} %constant.147.clone) | copy-start | bytes 28
  424.6 368.1 %all-gather.16.cloned.1.call-start = ((), (), s32[]{:S(2)}) async-start(), calls=%async_computation.16 | async-start | bytes 2506752 | tf_op jit(solution)/shard_map/all_gather | solution.py:282
  554.4 320.6 %all-gather.18.cloned.1.call-start = ((), (), s32[]{:S(2)}) async-start(), calls=%async_computation.17 | async-start | bytes 5013504 | tf_op jit(solution)/shard_map/all_gather | solution.py:285
  730.4 166.4 %all-gather.20.cloned.1.call-start = ((), (), s32[]{:S(2)}) async-start(), calls=%async_computation.18 | async-start | bytes 7077888 | tf_op jit(solution)/shard_map/all_gather | solution.py:86
  879.1 2.0 copy-start.35
  881.0 8.6 copy-start.33
  881.0 8.6 copy-start.6
  881.0 8.6 copy-start.9
  881.1 313.3 %all-reduce.7.cloned.1.call-start = ((), (), s32[]{:S(2)}) async-start(), calls=%async_computation.9 | async-start | bytes 2949120 | tf_op jit(solution)/shard_map/psum | solution.py:180
  889.5 350.4 %all-gather.14.cloned.1.call-start = ((), (), s32[]{:S(2)}) async-start(), calls=%async_computation.13 | async-start | bytes 2211840 | tf_op jit(solution)/shard_map/all_gather | solution.py:237
  892.6 430.7 %reduce-scatter.15.cloned.1.call-start = ((), (), s32[]{:S(2)}) async-start(), calls=%async_computation.19 | async-start | bytes 5013504 | tf_op jit(solution)/shard_map/reduce_scatter | solution.py:299
  896.8 38.8 %slice-start = ((s8[4718592]{0:T(1024)(128)(4,1)}), s8[524288]{0:T(1024)(128)(4,1)S(1)}, s32[]{:S(2)}) async-start(s8[4718592]{0:T(1024)(128)(4,1)} %bitcast.232), calls=%async_computation.21 | async-start | bytes 1048576
  903.0 32.6 %slice-start.1 = ((s8[4718592]{0:T(1024)(128)(4,1)}), s8[4194304]{0:T(1024)(128)(4,1)S(1)}, s32[]{:S(2)}) async-start(s8[4718592]{0:T(1024)(128)(4,1)} %bitcast.232), calls=%async_computation.22 | async-start | bytes 8388608
  1068.7 23.9 %copy-start.43 = (f32[768,3072]{1,0:T(8,128)}, f32[768,3072]{1,0:T(8,128)S(1)}, u32[]{:S(2)}) copy-start(f32[768,3072]{1,0:T(8,128)S(1)} %multiply_add_fusion.1) | copy-start | bytes 28311556
  1181.0 2.1 copy-start.2
  1185.9 313.3 %reduce-scatter.17.cloned.1.call-start = ((), (), s32[]{:S(2)}) async-start(), calls=%async_computation.20 | async-start | bytes 10027008 | tf_op jit(solution)/shard_map/reduce_scatter | solution.py:300
  1193.2 1.4 copy-start.1
  1193.2 1.9 copy-start.4
  1193.2 1.9 copy-start.27
  1195.1 3.2 copy-start.29
  1198.3 300.9 %copy-start.19 = (f32[48,2,1536]{2,1,0:T(2,128)S(1)}, f32[48,2,1536]{2,1,0:T(2,128)}, u32[]{:S(2)}) copy-start(f32[48,2,1536]{2,1,0:T(2,128)} %param.24) | copy-start | bytes 1769476
  1198.3 300.9 %copy-start.39 = (f32[2]{0:T(128)S(1)}, f32[2]{0:T(128)}, u32[]{:S(2)}) copy-start(f32[2]{0:T(128)} %constant.149.clone) | copy-start | bytes 28
  1241.7 260.1 %copy-start.20 = (bf16[960,768]{1,0:T(8,128)(2,1)S(1)}, bf16[960,768]{1,0:T(8,128)(2,1)}, u32[]{:S(2)}) copy-start(bf16[960,768]{1,0:T(8,128)(2,1)} %all-gather.14.cloned.1.call-done) | copy-start | bytes 4423684
Sparse Core Ops, SparseCore 0:
  11.3 61.1 all-gather.7
  132.0 21.4 all-reduce.4
  156.7 79.0 all-gather.9
  252.7 10.2 reduce-scatter.6
  269.8 10.8 all-gather.11
  364.5 10.1 reduce-scatter.8
  416.2 136.3 reduce-scatter.10
  559.2 169.0 reduce-scatter.12
  731.6 61.1 all-gather.15
  795.9 79.0 all-gather.17
  881.1 15.6 all-gather.19
  899.6 21.4 all-reduce.6
  922.6 10.8 all-gather.13
  1186.0 137.2 reduce-scatter.14
  1329.8 169.3 reduce-scatter.16
where the time goes:
time: 1520 us; the launch traced here: 1510 us
  waiting for transfers between devices  871 us (57%)
  matrix products  420 us (28%)
  other arithmetic  92.2 us (6%)
  local copies, waits for them, and re-layouts  54.4 us (4%)
  blocking collectives  44.1 us (3%)
  between operations  25.5 us (2%)
    reduce_scatter x1, waiting for transfers between devices, body(): lax.psum_scatter(mlp_back_rows, 'dp', scatter_dimension=0, tiled=True)  174 us
    reduce_scatter x1, waiting for transfers between devices, body(): lax.psum_scatter(mlp_grad, 'dp', scatter_dimension=0, tiled=True)  174 us
    dot_general x51, matrix products, contract(): lax.dot_general(left, right, (((left_dim,), (right_dim,)), ((), ())), pre...  130 us
    reduce_scatter x1, waiting for transfers between devices, body(): lax.psum_scatter(attn_grad, 'dp', scatter_dimension=0, tiled=True)  128 us
    dot_general x5, matrix products, newton(): jnp.dot(polynomial, current, precision=lax.Precision.HIGHEST)  124 us
    dot_general x5, matrix products, newton(): lax.dot_general(current, current, (((1,), (1,)), ((), ())), precision=lax...  123 us
    reduce_scatter x1, waiting for transfers between devices, body(): lax.psum_scatter(attn_back_rows, 'dp', scatter_dimension=0, tiled=True)  80.4 us
    all_gather x1, waiting for transfers between devices, body(): lax.all_gather(mlp_moment.astype(jnp.bfloat16), 'dp', axis=0, tiled=True)  79.9 us
  transfers between devices with their start and end apart: 15, of which 12 were waited for; matrix products, arithmetic and copies ran while one was open for 25% of the time, Pallas kernels for 0%

commit v1 on v0

v1 whole, which is shorter than its diff:
```python
import functools
import math

import jax
import jax.numpy as jnp
from jax import lax
from jax.experimental import pallas as pl
from jax.experimental.pallas import tpu as pltpu
from jax.sharding import PartitionSpec as P

D = 768
HD = 64
FF = 3072
LEN = 960
NS_ITERS = 5


COEF_A = 3.4445
COEF_B = -4.775
COEF_C = 2.0315


def gelu_tanh(values):
    return jax.nn.gelu(values, approximate=True)


def layer_norm(values, norm_gain, norm_bias):
    centered = values - jnp.mean(values, axis=-1, keepdims=True)
    inverse = lax.rsqrt(jnp.mean(centered * centered, axis=-1, keepdims=True) + 1e-05)
    normed = centered * inverse
    return (normed * norm_gain + norm_bias, normed, inverse)


def norm_back(grad_out, norm_gain, normed, inverse):
    scaled = grad_out * norm_gain
    return inverse * (
        scaled
        - jnp.mean(scaled, axis=-1, keepdims=True)
        - normed * jnp.mean(scaled * normed, axis=-1, keepdims=True)
    )


def contract(left, right, left_dim, right_dim):
    return lax.dot_general(
        left, right, (((left_dim,), (right_dim,)), ((), ())), preferred_element_type=jnp.float32
    )


MESH = pl.DeviceIdType.MESH
MIB = 1 << 20
LINE = 4
OWNERS = (7, 8, 6, 9, 4, 11)


def place():
    dp = lax.axis_index("dp")
    core = lax.axis_index("tensor")
    z = dp // 4
    y = dp % 4 // 2
    x = dp % 2
    return dp, core, z, y, x


def remote(src, dst, send, recv, dp, core):
    return pltpu.make_async_remote_copy(
        src_ref=src, dst_ref=dst, send_sem=send, recv_sem=recv, device_id=(dp, core), device_id_type=MESH
    )


def greet(barrier, dp, core):
    pl.semaphore_signal(barrier, inc=1, device_id=(dp, core), device_id_type=MESH)


def greet_all(dp, core, count, with_core):
    barrier = pltpu.get_barrier_semaphore()
    for step in range(1, count):
        greet(barrier, (dp + step) % count, core)
    if with_core:
        greet(barrier, dp, 1 - core)
    pl.semaphore_wait(barrier, count - 1 + int(with_core))


def scatter_kernel(rates, orth, attn, mlp, attn_new, mlp_new, attn_low, mlp_low, send, recv):
    dp, core, z, y, x = place()
    rows = attn.shape[0]
    count = orth.shape[0] // rows
    greet_all(dp, core, count, False)

    def at(ref, block):
        return ref.at[pl.ds(pl.multiple_of(block * rows, rows), rows)]

    def low_of(slot):
        return attn_low.at[slot] if slot < 4 else mlp_low.at[slot - 4]

    def size_of(slot):
        return attn.shape[2] if slot < 4 else mlp.shape[2]

    for slot in range(6):
        owner = OWNERS[slot]

        @pl.when(dp == owner)
        def _():
            for step in range(1, count):
                target = (owner + step) % count
                src = at(orth, target).at[:, 0 : size_of(slot)]
                remote(src, low_of(slot), send.at[target], recv.at[slot], target, core).start()
            pltpu.make_async_copy(
                at(orth, owner).at[:, 0 : size_of(slot)], low_of(slot), recv.at[slot]
            ).start()

    for slot in range(6):
        owner = OWNERS[slot]
        low = low_of(slot)

        @pl.when(dp != owner)
        def _():
            remote(low, low, send.at[0], recv.at[slot], owner, core).wait_recv()

        @pl.when(dp == owner)
        def _():
            pltpu.make_async_copy(low, low, recv.at[slot]).wait()

        @pl.loop(0, rows // 16)
        def _(i):
            part = pl.ds(pl.multiple_of(i * 16, 16), 16)
            step = rates[slot] * low[part, :].astype(jnp.float32)
            if slot < 4:
                attn_new[part, slot, :] = attn[part, slot, :] - step
            else:
                mlp_new[part, slot - 4, :] = mlp[part, slot - 4, :] - step

    for slot in range(6):
        owner = OWNERS[slot]

        @pl.when(dp == owner)
        def _():
            for step in range(1, count):
                target = (owner + step) % count
                src = at(orth, target).at[:, 0 : size_of(slot)]
                remote(src, low_of(slot), send.at[target], recv.at[slot], target, core).wait_send()


def scatter_rows(orth, attn, mlp, rates, collective_id):
    dma = pltpu.SemaphoreType.DMA
    count = lax.axis_size("dp")
    rows = attn.shape[0]
    vmem = pl.BlockSpec(memory_space=pltpu.VMEM)
    return pl.pallas_call(
        functools.partial(scatter_kernel, rates),
        out_shape=[
            jax.ShapeDtypeStruct(attn.shape, jnp.float32),
            jax.ShapeDtypeStruct(mlp.shape, jnp.float32),
        ],
        in_specs=[vmem] * 3,
        out_specs=[vmem] * 2,
        scratch_shapes=[
            pltpu.VMEM((4, rows, attn.shape[2]), jnp.bfloat16),
            pltpu.VMEM((2, rows, mlp.shape[2]), jnp.bfloat16),
            dma((count,)),
            dma((6,)),
        ],
        compiler_params=pltpu.CompilerParams(
            collective_id=collective_id, has_side_effects=True, vmem_limit_bytes=32 * MIB
        ),
        name="scatter_rows",
    )(orth, attn, mlp)


def head_mask(shape):
    return lax.broadcasted_iota(jnp.int32, shape, 1) < HD


def spans(length):
    return [(start, min(256, length - start)) for start in range(0, length, 256)]


def attend_forward(q_ref, k_ref, v_ref, o_ref, lse_ref, turned, value_turned, after=lambda head: None):
    length = q_ref.shape[0]
    value_turned[...] = v_ref[...].astype(jnp.float32).T.astype(jnp.bfloat16)
    keys = k_ref[...]
    for head in range(2):
        mine = head_mask(keys.shape) if head == 0 else ~head_mask(keys.shape)
        head_keys = jnp.where(mine, keys, jnp.zeros_like(keys))
        for start, size in spans(length):
            stop = start + size
            scores = contract(head_keys[0:stop], q_ref[start:stop, :], 1, 1)
            key_at = lax.broadcasted_iota(jnp.int32, (stop, size), 0)
            query_at = lax.broadcasted_iota(jnp.int32, (stop, size), 1) + start
            scores = jnp.where(key_at <= query_at, scores, -1e30)
            peak = jnp.max(scores, axis=0, keepdims=True)
            weights = jnp.exp(scores - peak)
            total = jnp.sum(weights, axis=0, keepdims=True)
            mixed = contract(
                value_turned[head * HD : (head + 1) * HD, 0:stop], weights.astype(jnp.bfloat16), 1, 0
            )
            turned[head * HD : (head + 1) * HD, start:stop] = mixed / total
            lse_ref[head : head + 1, start:stop] = peak + jnp.log(total)
        after(head)
    o_ref[...] = turned[...].T.astype(jnp.bfloat16)


def attend_backward(q_ref, k_ref, v_ref, o_ref, do_ref, lse_ref, dq_ref, dk_ref, dv_ref, turned):
    length = q_ref.shape[0]
    keys, values = k_ref[...], v_ref[...]
    key_turned = keys.astype(jnp.float32).T.astype(jnp.bfloat16)
    inner = (o_ref[...].astype(jnp.float32) * do_ref[...].astype(jnp.float32)).T
    mask = head_mask(keys.shape)
    turned[...] = jnp.zeros_like(turned)
    for start, size in spans(length):
        stop = start + size
        both_k, both_v = [], []
        for head in range(2):
            mine = mask[start:stop] if head == 0 else ~mask[start:stop]
            head_keys = jnp.where(mine, keys[start:stop], 0)
            head_values = jnp.where(mine, values[start:stop], 0)
            head_inner = jnp.sum(inner[head * HD : (head + 1) * HD, start:], axis=0, keepdims=True)
            scores = contract(head_keys, q_ref[start:, :], 1, 1)
            grad_prob = contract(head_values, do_ref[start:, :], 1, 1)
            key_at = lax.broadcasted_iota(jnp.int32, scores.shape, 0)
            query_at = lax.broadcasted_iota(jnp.int32, scores.shape, 1)
            scores = jnp.where(key_at <= query_at, scores, -1e30)
            prob = jnp.exp(scores - lse_ref[head : head + 1, start:])
            grad_scores = (prob * (grad_prob - head_inner)).astype(jnp.bfloat16)
            both_v.append(contract(prob.astype(jnp.bfloat16), do_ref[start:, :], 1, 0))
            both_k.append(contract(grad_scores, q_ref[start:, :], 1, 0))
            turned[head * HD : (head + 1) * HD, start:] += contract(
                key_turned[head * HD : (head + 1) * HD, start:stop], grad_scores, 1, 0
            )
        pick = mask[start:stop]
        dk_ref[start:stop, :] = jnp.where(pick, both_k[0], both_k[1]).astype(jnp.bfloat16)
        dv_ref[start:stop, :] = jnp.where(pick, both_v[0], both_v[1]).astype(jnp.bfloat16)
    dq_ref[...] = (turned[...].T * (1.0 / math.sqrt(HD))).astype(jnp.bfloat16)


def pairs_forward(queries, keys, values):
    length, width = queries.shape
    block = pl.BlockSpec((length, 2 * HD), lambda i: (0, i))
    stat = pl.BlockSpec((None, 2, length), lambda i: (i, 0, 0))
    return pl.pallas_call(
        attend_forward,
        grid=(width // (2 * HD),),
        out_shape=[
            jax.ShapeDtypeStruct((length, width), jnp.bfloat16),
            jax.ShapeDtypeStruct((width // (2 * HD), 2, length), jnp.float32),
        ],
        in_specs=[block] * 3,
        out_specs=[block, stat],
        scratch_shapes=[pltpu.VMEM((2 * HD, length), jnp.float32), pltpu.VMEM((2 * HD, length), jnp.bfloat16)],
        compiler_params=pltpu.CompilerParams(vmem_limit_bytes=48 * MIB),
        name="attend_forward",
    )(queries, keys, values)


def pairs_backward(queries, keys, values, attended, grad_attended, stats):
    length, width = queries.shape
    block = pl.BlockSpec((length, 2 * HD), lambda i: (0, i))
    stat = pl.BlockSpec((None, 2, length), lambda i: (i, 0, 0))
    return pl.pallas_call(
        attend_backward,
        grid=(width // (2 * HD),),
        out_shape=[jax.ShapeDtypeStruct((length, width), jnp.bfloat16)] * 3,
        in_specs=[block] * 5 + [stat],
        out_specs=[block] * 3,
        scratch_shapes=[pltpu.VMEM((2 * HD, length), jnp.float32)],
        compiler_params=pltpu.CompilerParams(vmem_limit_bytes=48 * MIB),
        name="attend_backward",
    )(queries, keys, values, attended, grad_attended, stats)


class Gathering:
    def __init__(self, a_ref, b_ref, a_out, b_out, send, recv, local):
        self.own = (a_ref, b_ref)
        self.outs = (a_out, b_out)
        self.send, self.recv, self.local = send, recv, local
        self.rows = a_ref.shape[0]
        self.dp, self.core, self.z, self.y, self.x = place()
        self.x_peer = self.dp + 1 - 2 * self.x
        self.y_peer = self.dp + 2 - 4 * self.y

    def block(self, side, index):
        return self.outs[side].at[pl.ds(pl.multiple_of(index * self.rows, self.rows), self.rows)]

    def copy(self, kind, side, index, own, target):
        src = self.own[side] if own else self.block(side, index)
        return remote(
            src, self.block(side, index), self.send.at[kind, index // 4], self.recv.at[side, index], target, self.core
        )

    def arrived(self, side, index):
        block = self.block(side, index)
        remote(block, block, self.send.at[0, 0], self.recv.at[side, index], self.dp, self.core).wait_recv()

    def at(self, level, y_off, x_off):
        y = self.y + y_off * (1 - 2 * self.y)
        x = self.x + x_off * (1 - 2 * self.x)
        return level * 4 + y * 2 + x

    def line(self, level, own, action):
        index = self.at(level, 0, 0)

        @pl.when((self.z < LINE - 1) & (level <= self.z))
        def _():
            for side in range(2):
                action(self.copy(side, side, index, own, self.dp + 4))

        @pl.when((self.z > 0) & (level >= self.z))
        def _():
            for side in range(2):
                action(self.copy(2 + side, side, index, own, self.dp - 4))

        for side in range(2):
            action(self.copy(4 + side, side, index, own, self.x_peer))
            action(self.copy(6 + side, side, index, own, self.y_peer))

    def relays(self, level):
        return (
            (0, self.at(level, 0, 1), self.copy(8, 0, self.at(level, 0, 1), False, self.y_peer)),
            (1, self.at(level, 1, 0), self.copy(9, 1, self.at(level, 1, 0), False, self.x_peer)),
        )

    def by_distance(self, distance, action):
        if distance == 0:
            action(self.z)
            return

        @pl.when(self.z >= distance)
        def _():
            action(self.z - distance)

        @pl.when(self.z + distance < LINE)
        def _():
            action(self.z + distance)

    def local_copies(self):
        return [
            pltpu.make_async_copy(self.own[side], self.block(side, self.dp), self.local.at[side]) for side in range(2)
        ]

    def begin(self):
        self.line(self.z, True, lambda copy: copy.start())
        for copy in self.local_copies():
            copy.start()

    def onward(self, distance):
        def action(level):
            for side in range(2):
                self.arrived(side, self.at(level, 0, 0))
            self.line(level, False, lambda copy: copy.start())

        self.by_distance(distance, action)

    def relay(self, distance):
        def action(level):
            for side, index, copy in self.relays(level):
                self.arrived(side, index)
                copy.start()

        self.by_distance(distance, action)

    def finish(self):
        for level in range(LINE):
            self.arrived(1, self.at(level, 0, 1))
            self.arrived(0, self.at(level, 1, 0))
            for side in range(2):
                self.arrived(side, self.at(level, 1, 1))
        for copy in self.local_copies():
            copy.wait()

    def drain(self):
        for level in range(LINE):
            self.line(level, False, lambda copy: copy.wait_send())
            for _, _, copy in self.relays(level):
                copy.wait_send()


def norm_tile(values, gain, bias):
    centered = values - jnp.mean(values, axis=-1, keepdims=True)
    inverse = lax.rsqrt(jnp.mean(centered * centered, axis=-1, keepdims=True) + 1e-05)
    return centered * inverse * gain + bias


def tiles(count, rows, action):
    @pl.loop(0, count // rows)
    def _(i):
        action(pl.ds(pl.multiple_of(i * rows, rows), rows))


def front_kernel(
    tokens, vec, qk_shard, vo_shard, f0_shard, f1_shard, p0_shard, p1_shard,
    qk_all, vo_all, f0, f1, p0, p1, first, q, k, v, o, lse, middle, second, act, slope,
    turned, mixed, partial, partial_other, pre,
    send, recv, local, swap_send, swap_recv,
):
    dp, core, z, y, x = place()
    length = tokens.shape[0]
    width = q.shape[1]
    chunk = length // 4
    barrier = pltpu.get_barrier_semaphore()
    greet(barrier, dp + 1 - 2 * x, core)
    greet(barrier, dp + 2 - 4 * y, core)
    greet(barrier, dp, 1 - core)

    @pl.when(z > 0)
    def _():
        greet(barrier, dp - 4, core)

    @pl.when(z < LINE - 1)
    def _():
        greet(barrier, dp + 4, core)

    pl.semaphore_wait(barrier, 3 + (z + 2) // 3 + (5 - z) // 3)

    rounds = [
        Gathering(a, b, a_out, b_out, send.at[i], recv.at[i], local.at[i])
        for i, (a, b, a_out, b_out) in enumerate(
            ((qk_shard, vo_shard, qk_all, vo_all), (f0_shard, f1_shard, f0, f1), (p0_shard, p1_shard, p0, p1))
        )
    ]
    rounds[0].begin()

    def norm_one(part):
        tile = norm_tile(tokens[part, :].astype(jnp.float32), vec[0:1, :], vec[1:2, :])
        first[part, :] = tile.astype(jnp.bfloat16)

    tiles(length, 16, norm_one)
    rounds[0].onward(1)
    rounds[0].relay(0)
    rounds[0].onward(2)
    rounds[0].relay(1)
    rounds[0].onward(3)
    rounds[0].relay(2)
    rounds[0].relay(3)
    rounds[1].begin()
    rounds[0].finish()

    mine = pl.ds(pl.multiple_of(core * width, width), width)
    scale = 1.0 / math.sqrt(HD)
    q[...] = ((contract(first[...], qk_all[:, 0:width], 1, 0) + vec[4:5, mine]) * scale).astype(jnp.bfloat16)
    k[...] = contract(first[...], qk_all[:, width:], 1, 0).astype(jnp.bfloat16)
    v[...] = (contract(first[...], vo_all[:, 0:width], 1, 0) + vec[5:6, mine]).astype(jnp.bfloat16)

    def step(index):
        if index == 1:
            rounds[1].onward(1)
            rounds[1].relay(0)
        if index == 2:
            rounds[1].onward(2)
            rounds[1].relay(1)
        if index == 3:
            rounds[1].onward(3)
            rounds[1].relay(2)
        if index == 4:
            rounds[1].relay(3)
            rounds[2].begin()
        if index == 6:
            rounds[2].onward(1)
            rounds[2].relay(0)
        if index == 7:
            rounds[2].onward(2)
            rounds[2].relay(1)
        if index == 8:
            rounds[2].onward(3)
            rounds[2].relay(2)
        if index == 9:
            rounds[2].relay(3)

    for pair in range(width // (2 * HD)):
        lanes = pl.ds(pair * 2 * HD, 2 * HD)
        attend_forward(
            q.at[:, lanes], k.at[:, lanes], v.at[:, lanes], o.at[:, lanes], lse.at[pair], turned, mixed,
            lambda head: step(2 * pair + head),
        )

    def swap_copy(i):
        part = pl.ds(i * chunk, chunk)
        return remote(partial.at[part], partial_other.at[part], swap_send.at[i], swap_recv.at[i], dp, 1 - core)

    for i in range(4):
        part = pl.ds(i * chunk, chunk)
        partial[part, :] = contract(o[part, :], vo_all[:, width:], 1, 1).astype(jnp.bfloat16)
        swap_copy(i).start()
    step(6)
    rounds[1].finish()
    for i in range(4):
        swap_copy(i).wait_recv()

        def norm_two(part):
            rows = pl.ds(pl.multiple_of(i * chunk + part.start, 16), part.size)
            total = partial[rows, :].astype(jnp.float32) + partial_other[rows, :].astype(jnp.float32)
            tile = tokens[rows, :].astype(jnp.float32) + total + vec[6:7, :]
            middle[rows, :] = tile
            second[rows, :] = norm_tile(tile, vec[2:3, :], vec[3:4, :]).astype(jnp.bfloat16)

        tiles(chunk, 16, norm_two)
        rows = pl.ds(i * chunk, chunk)
        for side, weight in enumerate((f0, f1)):
            pre[:, side * D : (side + 1) * D] = contract(second[rows, :], weight[...], 1, 0)

        def curve(part):
            rows = pl.ds(pl.multiple_of(i * chunk + part.start, 16), part.size)
            for side in range(2):
                columns = pl.ds(side * D, D)
                value = pre[part, columns] + vec[pl.ds(8 + 2 * core + side, 1), :]
                square = value * value
                root = math.sqrt(2.0 / math.pi)
                bent = jnp.tanh(value * (root + root * 0.044715 * square))
                half = 0.5 + 0.5 * bent
                act[rows, columns] = (value * half).astype(jnp.bfloat16)
                inner = root + (3.0 * root * 0.044715) * square
                slope[rows, columns] = (half + (0.5 * value) * (1.0 - bent * bent) * inner).astype(jnp.bfloat16)

        tiles(chunk, 16, curve)
        step(7 + i)
    rounds[2].finish()
    for i in range(4):
        swap_copy(i).wait_send()
    for gathering in rounds:
        gathering.drain()


def front(tokens, vec, shards, collective_id):
    dma = pltpu.SemaphoreType.DMA
    low = jnp.bfloat16
    count = lax.axis_size("dp")
    length = tokens.shape[0]
    width = shards[0].shape[1] // 2
    hidden = 2 * D
    shape = jax.ShapeDtypeStruct
    vmem = pl.BlockSpec(memory_space=pltpu.VMEM)
    return pl.pallas_call(
        front_kernel,
        out_shape=[shape((count * shard.shape[0], shard.shape[1]), low) for shard in shards]
        + [shape((length, D), low)]
        + [shape((length, width), low)] * 4
        + [
            shape((width // (2 * HD), 2, length), jnp.float32),
            shape((length, D), jnp.float32),
            shape((length, D), low),
            shape((length, hidden), low),
            shape((length, hidden), low),
        ],
        in_specs=[vmem] * 8,
        out_specs=[vmem] * 16,
        scratch_shapes=[
            pltpu.VMEM((2 * HD, length), jnp.float32),
            pltpu.VMEM((2 * HD, length), low),
            pltpu.VMEM((length, D), low),
            pltpu.VMEM((length, D), low),
            pltpu.VMEM((length // 4, hidden), jnp.float32),
            dma((3, 10, LINE)),
            dma((3, 2, count)),
            dma((3, 2)),
            dma((4,)),
            dma((4,)),
        ],
        compiler_params=pltpu.CompilerParams(
            collective_id=collective_id, has_side_effects=True, vmem_limit_bytes=56 * MIB
        ),
        name="front",
    )(tokens, vec, *shards)


def norm_back_tile(grad, gain, values):
    centered = values - jnp.mean(values, axis=-1, keepdims=True)
    inverse = lax.rsqrt(jnp.mean(centered * centered, axis=-1, keepdims=True) + 1e-05)
    normed = centered * inverse
    scaled = grad * gain
    back = inverse * (
        scaled
        - jnp.mean(scaled, axis=-1, keepdims=True)
        - normed * jnp.mean(scaled * normed, axis=-1, keepdims=True)
    )
    return back, normed


def shifted(part, start):
    return pl.ds(pl.multiple_of(start + part.start, 16), part.size)


def column_sum(value):
    return jnp.sum(value, axis=0, keepdims=True)


def mlp_back_kernel(
    cot, vec, f0, f1, p0, p1, vo, o, middle, second, act, slope,
    out, grad_mid, do, ga, gb, sums,
    du, partial, other, m_partial, m_other, low, turned, acc, swap_send, swap_recv,
):
    dp = lax.axis_index("dp")
    core = lax.axis_index("tensor")
    length = cot.shape[0]
    width = o.shape[1]
    chunk = length // 4
    barrier = pltpu.get_barrier_semaphore()
    greet(barrier, dp, 1 - core)
    pl.semaphore_wait(barrier, 1)
    acc[...] = jnp.zeros_like(acc)
    sums[...] = jnp.zeros_like(sums)

    def swap_copy(kind, i):
        part = pl.ds(i * chunk, chunk)
        src, dst = ((partial, other), (m_partial, m_other))[kind]
        return remote(src.at[part], dst.at[part], swap_send.at[kind, i], swap_recv.at[kind, i], dp, 1 - core)

    sides = ((0, f0, p0), (1, f1, p1))
    for i in range(4):
        rows = pl.ds(i * chunk, chunk)
        for side, _, weight in sides:
            columns = pl.ds(side * D, D)
            value = contract(cot[rows, :], weight[...], 1, 0) * slope[rows, columns].astype(jnp.float32)
            value = value.astype(jnp.bfloat16)
            du[rows, columns] = value
            sums[4 + side : 5 + side, :] += column_sum(value.astype(jnp.float32))
        partial[rows, :] = (
            contract(du[rows, 0:D], f0[...], 1, 1) + contract(du[rows, D:], f1[...], 1, 1)
        ).astype(jnp.bfloat16)
        swap_copy(0, i).start()
    for i in range(4):
        rows = pl.ds(i * chunk, chunk)
        m_partial[rows, :] = (
            contract(act[rows, 0:D], p0[...], 1, 1) + contract(act[rows, D:], p1[...], 1, 1)
        ).astype(jnp.bfloat16)
        swap_copy(1, i).start()

    def outer(left, right, target, start):
        size = right.shape[1]
        for block in range(D // 256):
            rows = pl.ds(block * 256, 256)
            value = contract(left[rows, :], right[...], 1, 0)
            target[rows, start : start + size] = value.astype(jnp.bfloat16)
            row = 6 if size == D else 7
            sums[row : row + 1, 0:size] += column_sum(value * value)

    turned[...] = cot[...].T
    for side in range(2):
        outer(turned, act.at[:, side * D : (side + 1) * D], gb, width + side * D)
    for i in range(4):
        swap_copy(0, i).wait_recv()

        def back(part):
            rows = shifted(part, i * chunk)
            grad = partial[rows, :].astype(jnp.float32) + other[rows, :].astype(jnp.float32)
            outgoing = cot[rows, :].astype(jnp.float32)
            value, normed = norm_back_tile(grad, vec[2:3, :], middle[rows, :])
            value = value + outgoing
            grad_mid[rows, :] = value
            low[rows, :] = value.astype(jnp.bfloat16)
            acc[0] += grad * normed
            acc[1] += grad
            acc[2] += value
            acc[3] += outgoing

        tiles(chunk, 16, back)
        rows = pl.ds(i * chunk, chunk)
        do[rows, :] = contract(low[rows, :], vo[:, width:], 1, 0).astype(jnp.bfloat16)
    for row in range(4):
        sums[row : row + 1, :] = column_sum(acc[row])
    turned[...] = low[...].T
    outer(turned, o, gb, 0)
    turned[...] = second[...].T
    for side in range(2):
        outer(turned, du.at[:, side * D : (side + 1) * D], ga, side * D)
    for i in range(4):
        swap_copy(1, i).wait_recv()

        def finish(part):
            rows = shifted(part, i * chunk)
            total = m_partial[rows, :].astype(jnp.float32) + m_other[rows, :].astype(jnp.float32)
            out[rows, :] = (middle[rows, :] + total + vec[7:8, :]).astype(jnp.bfloat16)

        tiles(chunk, 16, finish)
    for kind in range(2):
        for i in range(4):
            swap_copy(kind, i).wait_send()


def mlp_back(cot, vec, f0, f1, p0, p1, vo, o, middle, second, act, slope, collective_id):
    dma = pltpu.SemaphoreType.DMA
    low = jnp.bfloat16
    length, hidden = act.shape
    width = o.shape[1]
    shape = jax.ShapeDtypeStruct
    vmem = pl.BlockSpec(memory_space=pltpu.VMEM)
    return pl.pallas_call(
        mlp_back_kernel,
        out_shape=[
            shape((length, D), low),
            shape((length, D), jnp.float32),
            shape((length, width), low),
            shape((D, hidden), low),
            shape((D, width + hidden), low),
            shape((8, D), jnp.float32),
        ],
        in_specs=[vmem] * 12,
        out_specs=[vmem] * 6,
        scratch_shapes=[pltpu.VMEM((length, hidden), low)]
        + [pltpu.VMEM((length, D), low)] * 5
        + [pltpu.VMEM((D, length), low), pltpu.VMEM((4, 16, D), jnp.float32), dma((2, 4)), dma((2, 4))],
        compiler_params=pltpu.CompilerParams(
            collective_id=collective_id, has_side_effects=True, vmem_limit_bytes=56 * MIB
        ),
        name="mlp_back",
    )(cot, vec, f0, f1, p0, p1, vo, o, middle, second, act, slope)


def attn_back_kernel(
    noise_scale, batch, clip,
    tokens, vec, first, q, k, v, o, do, lse, qk_all, vo_all, grad_mid, ga_early, gb_early, sums, included,
    attn_mom, mlp_mom, attn_noise, mlp_noise,
    grad_in, attn_out, mlp_out, vec_out, owned,
    dqk, dv, ga_late, gb_late, head_turned, turned, partial, other, acc, square, factors,
    diag_a, diag_b, x_a, x_b, y_a, y_b, up_a, up_b, down_a, down_b, attn_low, mlp_low, vec_send, vec_recv,
    send, recv, vec_sems, gather_send, gather_recv, swap_send, swap_recv, small,
):
    dp, core, z, y, x = place()
    rows = attn_mom.shape[0]
    width = attn_mom.shape[2]
    wide = mlp_mom.shape[2]
    length = tokens.shape[0]
    chunk = length // 4
    x_peer, y_peer = dp + 1 - 2 * x, dp + 2 - 4 * y
    count = ga_early.shape[0] // rows
    z_near = dp + 4 - 8 * (z % 2)
    z_far = dp + 8 - 16 * (z // 2)
    late_a, late_b = ga_late.shape[1], gb_late.shape[1]
    owned[...] = jnp.zeros_like(owned)
    greet_all(dp, core, count, True)

    def at(ref, block):
        return ref.at[pl.ds(pl.multiple_of(block * rows, rows), rows)]

    def go(kind, level, src, dst, target):
        return remote(src, dst, send.at[kind, level], recv.at[kind, level], target, core)

    half = z // 2
    order = (3 - 3 * half, 2 - half, 1 - z + 4 * half, z)
    parts_a = ((0, late_a, ga_late), (late_a, ga_early.shape[1], ga_early))
    parts_b = ((0, late_b, gb_late), (late_b, gb_early.shape[1], gb_early))

    def x_block(level):
        return level * 4 + y * 2 + 1 - x

    def y_block(level):
        return level * 4 + (1 - y) * 2 + x

    def diag_copies(level, early):
        block = level * 4 + (1 - y) * 2 + 1 - x
        kind = 0 if early else 10
        start_a, size_a, grad_a = parts_a[early]
        start_b, size_b, grad_b = parts_b[early]
        return (
            go(kind, level, at(grad_a, block), diag_a.at[level, :, pl.ds(start_a, size_a)], y_peer),
            go(kind + 1, level, at(grad_b, block), diag_b.at[level, :, pl.ds(start_b, size_b)], x_peer),
        )

    def own_copies(level, early):
        kind = 2 if early else 12
        start_a, size_a, grad_a = parts_a[early]
        start_b, size_b, grad_b = parts_b[early]
        return (
            go(kind, level, at(grad_b, x_block(level)), x_b.at[level, :, pl.ds(start_b, size_b)], x_peer),
            go(kind + 1, level, at(grad_a, y_block(level)), y_a.at[level, :, pl.ds(start_a, size_a)], y_peer),
        )

    def sum_copies(level):
        return (
            go(4, level, diag_a.at[level], x_a.at[level], x_peer),
            go(5, level, diag_b.at[level], y_b.at[level], y_peer),
        )

    def up_copies(level):
        return (
            go(6, level, x_a.at[level], up_a.at[level], dp + 4),
            go(7, level, x_b.at[level], up_b.at[level], dp + 4),
        )

    def down_copies(level):
        return (
            go(8, level, x_a.at[level], down_a.at[level], dp - 4),
            go(9, level, x_b.at[level], down_b.at[level], dp - 4),
        )

    def small_copy(index):
        src, dst, target = (
            (square.at[0], square.at[1], (dp, 1 - core)),
            (factors.at[0], factors.at[1], (x_peer, core)),
            (factors.at[0], factors.at[2], (y_peer, core)),
        )[index]
        return remote(src, dst, small.at[0, index], small.at[1, index], *target)

    def vec_copy(stage):
        target = ((dp, 1 - core), (x_peer, core), (y_peer, core), (z_near, core), (z_far, core))[stage]
        return remote(vec_send.at[stage], vec_recv.at[stage], vec_sems.at[0, stage], vec_sems.at[1, stage], *target)

    def vec_step(stage):
        vec_copy(stage).wait_recv()
        total = vec_send[stage] + vec_recv[stage]
        if stage < 4:
            vec_send[stage + 1] = total
            vec_copy(stage + 1).start()
        else:
            vec_out[...] = total

    def swap_copy(i):
        part = pl.ds(i * chunk, chunk)
        return remote(partial.at[part], other.at[part], swap_send.at[i], swap_recv.at[i], dp, 1 - core)

    for level in order:
        for copy in diag_copies(level, 1):
            copy.start()
    for level in order:
        for copy in own_copies(level, 1):
            copy.start()

    acc[...] = jnp.zeros_like(acc)
    for pair in range(width // (2 * HD)):
        lanes = pl.ds(pair * 2 * HD, 2 * HD)
        attend_backward(
            q.at[:, lanes], k.at[:, lanes], v.at[:, lanes], o.at[:, lanes], do.at[:, lanes], lse.at[pair],
            dqk.at[:, lanes], dqk.at[:, pl.ds(width + pair * 2 * HD, 2 * HD)], dv.at[:, lanes], head_turned,
        )
    for i in range(4):
        part = pl.ds(i * chunk, chunk)
        partial[part, :] = (
            contract(dqk[part, :], qk_all[...], 1, 1) + contract(dv[part, :], vo_all[:, 0:width], 1, 1)
        ).astype(jnp.bfloat16)
        swap_copy(i).start()
    turned[...] = first[...].T
    squares = jnp.zeros((1, 1), jnp.float32)
    for right, target in ((dqk, ga_late), (dv, gb_late)):
        for block in range(D // 256):
            part = pl.ds(block * 256, 256)
            value = contract(turned[part, :], right[...], 1, 0)
            target[part, :] = value.astype(jnp.bfloat16)
            squares = squares + jnp.sum(column_sum(value * value), axis=1, keepdims=True)
    for level in order:
        for copy in diag_copies(level, 0):
            copy.start()
    for level in order:
        for copy in own_copies(level, 0):
            copy.start()
    bias_q = column_sum(dqk[:, 0:width].astype(jnp.float32))
    bias_v = column_sum(dv[...].astype(jnp.float32))
    for value in (sums[6:7, :], sums[7:8, :]):
        squares = squares + jnp.sum(value, axis=1, keepdims=True)
    for value in (bias_q, bias_v, sums[4:5, :], sums[5:6, :]):
        squares = squares + jnp.sum(value * value, axis=1, keepdims=True)
    square[0] = jnp.broadcast_to(squares, square.shape[1:])
    small_copy(0).start()

    for i in range(4):
        swap_copy(i).wait_recv()

        def back(part):
            here = shifted(part, i * chunk)
            grad = partial[here, :].astype(jnp.float32) + other[here, :].astype(jnp.float32)
            value, normed = norm_back_tile(grad, vec[0:1, :], tokens[here, :].astype(jnp.float32))
            grad_in[here, :] = (grad_mid[here, :] + value).astype(jnp.bfloat16)
            acc[0] += grad * normed
            acc[1] += grad

        tiles(chunk, 16, back)
    gain_one, bias_one = column_sum(acc[0]), column_sum(acc[1])
    shared = jnp.zeros((1, 1), jnp.float32)
    for value in (gain_one, bias_one, sums[0:1, :], sums[1:2, :], sums[2:3, :], sums[3:4, :]):
        shared = shared + jnp.sum(value * value, axis=1, keepdims=True)
    small_copy(0).wait_recv()
    norm = jnp.sqrt(square[0, 0:1, 0:1] + square[1, 0:1, 0:1] + shared)
    factor = included[0:1, 0:1] * jnp.minimum(1.0, clip / (norm + 1e-06))
    factors[0] = jnp.broadcast_to(factor, factors.shape[1:])
    small_copy(1).start()
    small_copy(2).start()
    leading = factor * (1 - core).astype(jnp.float32)
    vec_send[0] = jnp.zeros(vec_send.shape[1:], jnp.float32)
    mine = pl.ds(pl.multiple_of(core * width, width), width)
    for row, value in ((0, gain_one), (1, bias_one), (2, sums[0:1, :]), (3, sums[1:2, :]), (6, sums[2:3, :]), (7, sums[3:4, :])):
        vec_send[0, row : row + 1, :] = leading * value
    vec_send[0, 4:5, mine] = factor * bias_q
    vec_send[0, 5:6, mine] = factor * bias_v
    vec_send[0, pl.ds(8 + 2 * core, 1), :] = factor * sums[4:5, :]
    vec_send[0, pl.ds(9 + 2 * core, 1), :] = factor * sums[5:6, :]
    vec_copy(0).start()
    small_copy(1).wait_recv()
    small_copy(2).wait_recv()
    factor_x, factor_y = factors[1, 0:1, 0:1], factors[2, 0:1, 0:1]

    def weigh(dst, parts, block, scale_dst, terms):
        @pl.loop(0, rows // 16)
        def _(i):
            part = pl.ds(pl.multiple_of(i * 16, 16), 16)
            for start, size, grad in parts:
                columns = pl.ds(start, size)
                own = grad[pl.ds(pl.multiple_of(block * rows + i * 16, 16), 16), :].astype(jnp.float32)
                total = factor * own
                for scale, ref in ((scale_dst, dst),) + terms:
                    value = ref[part, columns].astype(jnp.float32)
                    total = total + (value if scale is None else scale * value)
                dst[part, columns] = total.astype(dst.dtype)

    vec_step(0)
    for level in order:
        to_x, to_y = sum_copies(level)
        for early in range(2):
            wait_a, wait_b = diag_copies(level, early)
            wait_a.wait_recv()
            wait_b.wait_recv()
        weigh(diag_a.at[level], parts_a, x_block(level), factor_y, ())
        to_x.start()
        weigh(diag_b.at[level], parts_b, y_block(level), factor_x, ())
        to_y.start()
    vec_step(1)

    def arrivals(level):
        for copy in own_copies(level, 0) + own_copies(level, 1) + sum_copies(level):
            copy.wait_recv()

    for index in range(3):
        level = order[index]
        block = level * 4 + y * 2 + x
        arrivals(level)

        def combine(extra_a, extra_b):
            weigh(x_a.at[level], parts_a, block, None, ((factor_y, y_a.at[level]),) + extra_a)
            weigh(x_b.at[level], parts_b, block, factor_x, ((None, y_b.at[level]),) + extra_b)

        @pl.when(level > z)
        def _():
            @pl.when(z > 0)
            def _():
                for copy in up_copies(level):
                    copy.wait_recv()
                combine(((None, up_a.at[level]),), ((None, up_b.at[level]),))

            @pl.when(z == 0)
            def _():
                combine((), ())

            for copy in up_copies(level):
                copy.start()

        @pl.when(level < z)
        def _():
            @pl.when(z < LINE - 1)
            def _():
                for copy in down_copies(level):
                    copy.wait_recv()
                combine(((None, down_a.at[level]),), ((None, down_b.at[level]),))

            @pl.when(z == LINE - 1)
            def _():
                combine((), ())

            for copy in down_copies(level):
                copy.start()

        vec_step(2 + index)
    arrivals(z)

    @pl.when(z > 0)
    def _():
        for copy in up_copies(z):
            copy.wait_recv()

    @pl.when(z == 0)
    def _():
        up_a[0] = jnp.zeros(up_a.shape[1:], up_a.dtype)
        up_b[0] = jnp.zeros(up_b.shape[1:], up_b.dtype)

    @pl.when(z < LINE - 1)
    def _():
        for copy in down_copies(z):
            copy.wait_recv()

    @pl.when(z == LINE - 1)
    def _():
        down_a[LINE - 1] = jnp.zeros(down_a.shape[1:], down_a.dtype)
        down_b[LINE - 1] = jnp.zeros(down_b.shape[1:], down_b.dtype)

    side_a = ((None, x_a), (factor_y, y_a), (None, up_a), (None, down_a))
    side_b = ((factor_x, x_b), (None, y_b), (None, up_b), (None, down_b))
    pieces = (
        (4, side_a, 2 * width, ga_early, 0),
        (5, side_b, 2 * width, gb_early, width),
        (0, side_a, 0, ga_late, 0),
        (1, side_a, width, ga_late, width),
        (2, side_b, 0, gb_late, 0),
        (3, side_b, width, gb_early, 0),
    )
    for slot, terms, column, grad, grad_column in pieces:
        size = width if slot < 4 else wide
        columns = pl.ds(column, size)
        low = attn_low.at[slot] if slot < 4 else mlp_low.at[slot - 4]

        @pl.loop(0, rows // 16)
        def _(i):
            part = pl.ds(pl.multiple_of(i * 16, 16), 16)
            own = grad[pl.ds(pl.multiple_of(dp * rows + i * 16, 16), 16), pl.ds(grad_column, size)]
            total = factor * own.astype(jnp.float32)
            for scale, ref in terms:
                value = ref[z, part, columns].astype(jnp.float32)
                total = total + (value if scale is None else scale * value)
            if slot < 4:
                moment = 0.5 * attn_mom[part, slot, :] + (total + noise_scale * attn_noise[part, slot, :]) / batch
                attn_out[part, slot, :] = moment
            else:
                moment = 0.5 * mlp_mom[part, slot - 4, :] + (total + noise_scale * mlp_noise[part, slot - 4, :]) / batch
                mlp_out[part, slot - 4, :] = moment
            low[part, :] = moment.astype(low.dtype)

        owner = OWNERS[slot]
        target = at(owned, dp).at[:, 0:size]

        @pl.when(dp != owner)
        def _():
            remote(low, target, gather_send.at[slot], gather_recv.at[dp], owner, core).start()

        @pl.when(dp == owner)
        def _():
            pltpu.make_async_copy(low, target, gather_send.at[slot]).start()

    for slot in range(6):
        size = width if slot < 4 else wide
        low = attn_low.at[slot] if slot < 4 else mlp_low.at[slot - 4]
        owner = OWNERS[slot]

        @pl.when(dp != owner)
        def _():
            remote(low, low, gather_send.at[slot], gather_recv.at[dp], owner, core).wait_send()

        @pl.when(dp == owner)
        def _():
            pltpu.make_async_copy(low, at(owned, dp).at[:, 0:size], gather_send.at[slot]).wait()
            for source in range(count):
                if source != owner:
                    block = at(owned, source).at[:, 0:size]
                    remote(block, block, gather_send.at[slot], gather_recv.at[source], source, core).wait_recv()

    for index in range(3):
        small_copy(index).wait_send()
    for i in range(4):
        swap_copy(i).wait_send()
    for stage in range(5):
        vec_copy(stage).wait_send()
    for level in range(LINE):
        for early in range(2):
            for copy in diag_copies(level, early) + own_copies(level, early):
                copy.wait_send()
        for copy in sum_copies(level):
            copy.wait_send()

        @pl.when(level > z)
        def _():
            for copy in up_copies(level):
                copy.wait_send()

        @pl.when(level < z)
        def _():
            for copy in down_copies(level):
                copy.wait_send()


def attn_back(
    tokens, vec, first, q, k, v, o, do, lse, qk_all, vo_all, grad_mid, ga_early, gb_early, sums, included,
    attn_mom, mlp_mom, attn_noise, mlp_noise, noise_scale, batch, clip, collective_id,
):
    dma = pltpu.SemaphoreType.DMA
    low = jnp.bfloat16
    count = lax.axis_size("dp")
    length = tokens.shape[0]
    rows, _, width = attn_mom.shape
    wide = mlp_mom.shape[2]
    side = 2 * width + wide
    shape = jax.ShapeDtypeStruct
    vmem = pl.BlockSpec(memory_space=pltpu.VMEM)
    scratch = pltpu.VMEM
    return pl.pallas_call(
        functools.partial(attn_back_kernel, noise_scale, batch, clip),
        out_shape=[
            shape((length, D), low),
            shape(attn_mom.shape, jnp.float32),
            shape(mlp_mom.shape, jnp.float32),
            shape(vec.shape, jnp.float32),
            shape((D, wide), low),
        ],
        in_specs=[vmem] * 20,
        out_specs=[vmem] * 5,
        scratch_shapes=[
            scratch((length, 2 * width), low),
            scratch((length, width), low),
            scratch((D, 2 * width), low),
            scratch((D, width), low),
            scratch((2 * HD, length), jnp.float32),
            scratch((D, length), low),
            scratch((length, D), low),
            scratch((length, D), low),
            scratch((2, 16, D), jnp.float32),
            scratch((2, 8, 128), jnp.float32),
            scratch((3, 8, 128), jnp.float32),
        ]
        + [scratch((LINE, rows, side), low)] * 10
        + [
            scratch((4, rows, width), low),
            scratch((2, rows, wide), low),
            scratch((5,) + vec.shape, jnp.float32),
            scratch((5,) + vec.shape, jnp.float32),
            dma((14, LINE)),
            dma((14, LINE)),
            dma((2, 5)),
            dma((6,)),
            dma((count,)),
            dma((4,)),
            dma((4,)),
            dma((2, 3)),
        ],
        compiler_params=pltpu.CompilerParams(
            collective_id=collective_id, has_side_effects=True, vmem_limit_bytes=60 * MIB
        ),
        name="attn_back",
    )(
        tokens, vec, first, q, k, v, o, do, lse, qk_all, vo_all, grad_mid, ga_early, gb_early, sums, included,
        attn_mom, mlp_mom, attn_noise, mlp_noise,
    )


def placed(piece, start, total_size):
    return lax.dynamic_update_slice_in_dim(jnp.zeros((total_size,), jnp.float32), piece, start, 0)


def other_core(value):
    return lax.ppermute(value, "tensor", [(0, 1), (1, 0)])


def newton(owned):
    gram = contract(owned, owned, 1, 1)
    gram = gram + other_core(gram)
    rows = gram.shape[0]
    diagonal = lax.broadcasted_iota(jnp.int32, (rows, rows), 0) == lax.broadcasted_iota(
        jnp.int32, (rows, rows), 1
    )
    scale = 1.0 / (jnp.sqrt(jnp.sum(jnp.where(diagonal, gram, 0.0))) + 1e-07)
    current = gram * (scale * scale)

    def product(left, right, fine):
        if fine:
            return jnp.dot(left, right, precision=lax.Precision.HIGH)
        return contract(left.astype(jnp.bfloat16), right.astype(jnp.bfloat16), 1, 0)

    factor = None
    for iteration in range(NS_ITERS):
        fine = iteration >= NS_ITERS - 2
        rest = COEF_B * current + COEF_C * product(current, current, fine)
        if factor is None:
            factor = jnp.where(diagonal, COEF_A, 0.0) + rest
        else:
            factor = COEF_A * factor + product(rest, factor, fine)
        if iteration < NS_ITERS - 1:
            once = COEF_A * current + product(rest, current, fine)
            current = COEF_A * once + product(rest, once, fine)
    return contract((factor * scale).astype(jnp.bfloat16), owned, 1, 0).astype(jnp.bfloat16)


def body(
    fast,
    tokens,
    cotangent,
    inclusion,
    attn_weights,
    mlp_weights,
    attn_momentum,
    mlp_momentum,
    attn_noise,
    mlp_noise,
    vectors,
    vector_momentum,
    vector_noise,
):
    dp_count = lax.axis_size("dp")
    dp_index = lax.axis_index("dp")
    halves = lax.axis_size("tensor")
    tensor_index = lax.axis_index("tensor")
    head_width = D // halves
    hidden_width = FF // halves
    query_scale = 1.0 / math.sqrt(HD)
    clip = 1.5 * D * math.sqrt(LEN)
    sigma = 0.05 * math.sqrt(dp_count) / D
    batch = 0.75 * dp_count
    attn_shard = attn_weights.astype(jnp.bfloat16)
    mlp_shard = mlp_weights.astype(jnp.bfloat16)
    rows = attn_shard.shape[0]
    shards = (
        attn_shard[:, 0:2].reshape(rows, 2 * head_width),
        attn_shard[:, 2:4].reshape(rows, 2 * head_width),
        mlp_shard[:, 0, 0:D],
        mlp_shard[:, 0, D:],
        mlp_shard[:, 1, 0:D],
        mlp_shard[:, 1, D:],
    )
    noise_scale = sigma * clip
    if fast:
        vec = vectors.reshape(-1, D)
        (
            query_key, value_out, fc_one, fc_two, pr_one, pr_two,
            first_low, queries, key_rows, value_rows, attended_low, stats, middle, second_low, activation_low, slope,
        ) = front(tokens[0], vec, shards, 0)
        result, grad_mid, grad_attended, early_a, early_b, sums = mlp_back(
            cotangent[0], vec, fc_one, fc_two, pr_one, pr_two, value_out, attended_low, middle, second_low,
            activation_low, slope, 1,
        )
        grad_in, attn_moment, mlp_moment, vector_summed, owned = attn_back(
            tokens[0], vec, first_low, queries, key_rows, value_rows, attended_low, grad_attended, stats,
            query_key, value_out, grad_mid, early_a, early_b, sums,
            jnp.broadcast_to(inclusion[0].astype(jnp.float32), (8, 128)),
            attn_momentum, mlp_momentum, attn_noise, mlp_noise, noise_scale, batch, clip, 2,
        )
        vector_summed = vector_summed.reshape(-1)
    else:
        gain_one = vectors[0:D]
        bias_one = vectors[D : 2 * D]
        gain_two = vectors[2 * D : 3 * D]
        bias_two = vectors[3 * D : 4 * D]
        query_bias = lax.dynamic_slice_in_dim(vectors, 4 * D + tensor_index * head_width, head_width)
        value_bias = lax.dynamic_slice_in_dim(vectors, 5 * D + tensor_index * head_width, head_width)
        attn_bias = vectors[6 * D : 7 * D]
        mlp_bias = vectors[7 * D : 8 * D]
        hidden_bias = lax.dynamic_slice_in_dim(
            vectors, 8 * D + tensor_index * hidden_width, hidden_width
        )
        inputs = tokens[0].astype(jnp.float32)
        length = inputs.shape[0]
        first, normed_one, inverse_one = layer_norm(inputs, gain_one, bias_one)

        def both_cores(partial):
            low = partial.astype(jnp.bfloat16)
            return low.astype(jnp.float32) + other_core(low).astype(jnp.float32)

        query_key, value_out, fc_one, fc_two, pr_one, pr_two = (
            lax.all_gather(shard, "dp", axis=0, tiled=True) for shard in shards
        )
        value_weight, out_weight = value_out[:, 0:head_width], value_out[:, head_width:]
        first_low = first.astype(jnp.bfloat16)
        qk = contract(first_low, query_key, 1, 0)
        queries = ((qk[:, 0:head_width] + query_bias) * query_scale).astype(jnp.bfloat16)
        key_rows = qk[:, head_width:].astype(jnp.bfloat16)
        value_rows = (contract(first_low, value_weight, 1, 0) + value_bias).astype(jnp.bfloat16)
        attended_low, stats = pairs_forward(queries, key_rows, value_rows)
        middle = inputs + both_cores(contract(attended_low, out_weight, 1, 1)) + attn_bias
        second_low = layer_norm(middle, gain_two, bias_two)[0].astype(jnp.bfloat16)
        pre_act = contract(second_low, jnp.concatenate([fc_one, fc_two], axis=1), 1, 0) + hidden_bias
        activation, gelu_back = jax.vjp(gelu_tanh, pre_act)
        activation_low = activation.astype(jnp.bfloat16)
        slope = gelu_back(jnp.ones_like(pre_act))[0]
        _, normed_two, inverse_two = layer_norm(middle, gain_two, bias_two)
        fc_weight = jnp.concatenate([fc_one, fc_two], axis=1)
        pr_weight = jnp.concatenate([pr_one, pr_two], axis=1)
        result = middle + both_cores(contract(activation_low, pr_weight, 1, 1)) + mlp_bias
        cot_low = cotangent[0]
        grad_out = cot_low.astype(jnp.float32)
        d_pr = contract(cot_low, activation_low, 0, 0)
        grad_pre = (contract(cot_low, pr_weight, 1, 0) * slope.astype(jnp.float32)).astype(jnp.bfloat16)
        d_fc = contract(second_low, grad_pre, 0, 0)
        d_hidden_bias = jnp.sum(grad_pre.astype(jnp.float32), axis=0)
        grad_two = both_cores(contract(grad_pre, fc_weight, 1, 1))
        grad_mid = grad_out + norm_back(grad_two, gain_two, normed_two, inverse_two)
        d_gain_two = jnp.sum(grad_two * normed_two, axis=0)
        d_bias_two = jnp.sum(grad_two, axis=0)
        d_attn_bias = jnp.sum(grad_mid, axis=0)
        d_mlp_bias = jnp.sum(grad_out, axis=0)
        mid_low = grad_mid.astype(jnp.bfloat16)
        d_out = contract(mid_low, attended_low, 0, 0)
        grad_attended = contract(mid_low, out_weight, 1, 0).astype(jnp.bfloat16)
        grad_q, grad_k, grad_v = pairs_backward(
            queries, key_rows, value_rows, attended_low, grad_attended, stats
        )
        grad_qk = jnp.concatenate([grad_q, grad_k], axis=1)
        d_query_key = contract(first_low, grad_qk, 0, 0)
        d_value = contract(first_low, grad_v, 0, 0)
        d_query_bias = jnp.sum(grad_q.astype(jnp.float32), axis=0)
        d_value_bias = jnp.sum(grad_v.astype(jnp.float32), axis=0)
        grad_one = both_cores(contract(grad_qk, query_key, 1, 1) + contract(grad_v, value_weight, 1, 1))
        grad_in = grad_mid + norm_back(grad_one, gain_one, normed_one, inverse_one)
        d_gain_one = jnp.sum(grad_one * normed_one, axis=0)
        d_bias_one = jnp.sum(grad_one, axis=0)
        split_square = sum(
            jnp.sum(value * value)
            for value in (d_query_key, d_value, d_out, d_fc, d_pr, d_query_bias, d_value_bias, d_hidden_bias)
        )
        split_tile = jnp.broadcast_to(split_square, (8, 128))
        total_square = (split_tile + other_core(split_tile))[0, 0] + sum(
            jnp.sum(value * value)
            for value in (d_gain_one, d_bias_one, d_gain_two, d_bias_two, d_attn_bias, d_mlp_bias)
        )
        factor = inclusion[0].astype(jnp.float32) * jnp.minimum(
            1.0, clip / (jnp.sqrt(total_square) + 1e-06)
        )
        leading = (tensor_index == 0).astype(jnp.float32)
        vector_grad = (
            jnp.concatenate(
                [
                    leading * d_gain_one,
                    leading * d_bias_one,
                    leading * d_gain_two,
                    leading * d_bias_two,
                    placed(d_query_bias, tensor_index * head_width, D),
                    placed(d_value_bias, tensor_index * head_width, D),
                    leading * d_attn_bias,
                    leading * d_mlp_bias,
                    placed(d_hidden_bias, tensor_index * hidden_width, FF),
                ]
            )
            * factor
        )
        result, grad_in = result.astype(jnp.bfloat16), grad_in.astype(jnp.bfloat16)
        attn_grad = jnp.concatenate([d_query_key, d_value, d_out], axis=1) * factor
        mlp_grad = jnp.stack([d_fc, d_pr], axis=1) * factor
        attn_summed = lax.psum_scatter(attn_grad, "dp", scatter_dimension=0, tiled=True)
        mlp_summed = lax.psum_scatter(mlp_grad, "dp", scatter_dimension=0, tiled=True)
        attn_summed = attn_summed.reshape(rows, 4, head_width)
        vector_summed = lax.psum(vector_grad, ("dp", "tensor"))
        attn_moment = 0.5 * attn_momentum + (attn_summed + noise_scale * attn_noise) / batch
        mlp_moment = 0.5 * mlp_momentum + (mlp_summed + noise_scale * mlp_noise) / batch
        owners = jnp.array([slot * dp_count // 6 for slot in range(6)])
        full_attn = lax.all_gather(attn_moment.astype(jnp.bfloat16), "dp", axis=0, tiled=True)
        full_mlp = lax.all_gather(mlp_moment.astype(jnp.bfloat16), "dp", axis=0, tiled=True)
        attn_pick = (owners[0:4] == dp_index)[None, :, None]
        mlp_pick = (owners[4:6] == dp_index)[None, :, None]
        mine_attn = jnp.sum(jnp.where(attn_pick, full_attn, 0), axis=1)
        mine_mlp = jnp.sum(jnp.where(mlp_pick, full_mlp, 0), axis=1)
        owned = jnp.pad(mine_attn, ((0, 0), (0, hidden_width - head_width))) + mine_mlp
    vector_moment = 0.5 * vector_momentum + (vector_summed + noise_scale * vector_noise) / batch
    vector_rate = 0.2 * math.sqrt(dp_count / LEN)
    vectors_new = vectors - vector_rate * vector_moment
    orthogonal = newton(owned)
    rates = (0.5, 0.5, 0.5, 0.5 * max(1.0, math.sqrt(LEN) / 8.0), 0.5 * math.sqrt(FF / D), 0.5)
    if fast:
        attn_new, mlp_new = scatter_rows(orthogonal, attn_weights, mlp_weights, rates, 3)
    else:
        attn_rows = jnp.where(attn_pick, orthogonal[:, None, 0:head_width], 0)
        mlp_rows = jnp.where(mlp_pick, orthogonal[:, None, :], 0)
        attn_orth = lax.psum_scatter(attn_rows, "dp", scatter_dimension=0, tiled=True)
        mlp_orth = lax.psum_scatter(mlp_rows, "dp", scatter_dimension=0, tiled=True)
        attn_new = attn_weights - jnp.array(rates[0:4])[None, :, None] * attn_orth
        mlp_new = mlp_weights - jnp.array(rates[4:6])[None, :, None] * mlp_orth
    return (
        result[None],
        grad_in[None],
        attn_moment,
        mlp_moment,
        attn_new,
        mlp_new,
        vector_moment,
        vectors_new,
    )


def solution(mesh):
    fast = mesh.shape["dp"] == 16 and mesh.shape["tensor"] == 2
    in_specs = (
        P("dp", None, None),
        P("dp", None, None),
        P("dp"),
        P("dp", None, "tensor"),
        P("dp", None, "tensor"),
        P("dp", None, "tensor"),
        P("dp", None, "tensor"),
        P("dp", None, "tensor"),
        P("dp", None, "tensor"),
        P(),
        P(),
        P(),
    )
    out_specs = (
        P("dp", None, None),
        P("dp", None, None),
        P("dp", None, "tensor"),
        P("dp", None, "tensor"),
        P("dp", None, "tensor"),
        P("dp", None, "tensor"),
        P(),
        P(),
    )
    return jax.shard_map(
        functools.partial(body, fast), mesh=mesh, in_specs=in_specs, out_specs=out_specs, check_vma=False
    )
```

time: 1520 us -> 355 us (0.23)
  waiting for transfers between devices: 871 us -> 3.29 us
  matrix products: 420 us -> 37.9 us
  Pallas kernels: 0 us -> 288 us
  other arithmetic: 92.2 us -> 5.09 us
  blocking collectives: 44.1 us -> 0 us
  local copies, waits for them, and re-layouts: 54.4 us -> 11.1 us
  between operations: 25.5 us -> 2.61 us
    reduce_scatter x6 -> x0, waiting for transfers between devices: 563 us -> none  [the longest x1 174 us: body(): lax.psum_scatter(mlp_back_rows, 'dp', scatter_dimension=0, tiled=True)]
    all_gather x7 -> x0, waiting for transfers between devices: 289 us -> none  [the longest x1 79.9 us: body(): lax.all_gather(mlp_moment.astype(jnp.bfloat16), 'dp', axis=0, tiled=True)]
    pallas_call x0 -> x4, Pallas kernels: none -> 288 us  [the longest x1 110 us: attn_back(): pl.pallas_call(functools.partial(attn_back_kernel, noise_scale, batch, cl...]
    dot_general x18 -> x6, matrix products: 290 us -> 19 us  [product(): return jnp.dot(left, right, precision=lax.Precision.HIGH)]
    dot_general x51 -> x13, matrix products: 130 us -> 18.9 us  [contract(): lax.dot_general(left, right, (((left_dim,), (right_dim,)), ((), ())), pre...]
    psum x2 -> x0, blocking collectives: 44.1 us -> none  [the longest x1 40.1 us: body(): vector_summed = lax.psum(vector_grad, ('dp', 'tensor'))]
    reduce_sum x20 -> x1, other arithmetic: 29.6 us -> 3.28 us  [newton(): scale = 1.0 / (jnp.sqrt(jnp.sum(jnp.where(diagonal, gram, 0.0))) + 1e-07)]
    psum x2 -> x0, waiting for transfers between devices: 19.7 us -> none  [the longest x1 19.7 us: body(): lax.psum(contract(attended_low, out_weight, 1, 1).astype(jnp.bfloat16), '...]
  transfers between devices with their start and end apart: 15 -> 1, of which waited for: 12 -> 1; matrix products, arithmetic and copies ran while one was open for 25% -> 0% of each run, Pallas kernels for 0% -> 0%
where the time goes in v1:
time: 355 us; the launch traced here: 349 us
  Pallas kernels  288 us (81%)
  matrix products  37.9 us (11%)
  local copies, waits for them, and re-layouts  11.1 us (3%)
  other arithmetic  5.09 us (1%)
    pallas_call x1, Pallas kernels, attn_back(): pl.pallas_call(functools.partial(attn_back_kernel, noise_scale, batch, cl...  110 us
    pallas_call x1, Pallas kernels, front(): pl.pallas_call(front_kernel, out_shape=[shape((count * shard.shape[0], sh...  88.4 us
    pallas_call x1, Pallas kernels, mlp_back(): pl.pallas_call(mlp_back_kernel, out_shape=[shape((length, D), low), shape...  46.4 us
    pallas_call x1, Pallas kernels, scatter_rows(): pl.pallas_call(functools.partial(scatter_kernel, rates), out_shape=[jax.S...  44.1 us
    dot_general x6, matrix products, product(): return jnp.dot(left, right, precision=lax.Precision.HIGH)  19 us
    dot_general x13, matrix products, contract(): lax.dot_general(left, right, (((left_dim,), (right_dim,)), ((), ())), pre...  18.9 us
    unnamed x33, local copies, waits for them, and re-layouts  8.28 us
  transfers between devices with their start and end apart: 1, of which 1 were waited for; matrix products, arithmetic and copies ran while one was open for 0% of the time, Pallas kernels for 0%

profile of v1, /device:TPU:30, one launch (start us, length us, event | category | flops | bytes accessed | tf_op | source)
XLA Modules:
  0.0 348.5 jit_solution(16443441081285328709)
XLA Ops:
  0.6 1.2 copy.25
  1.8 0.7 slice_bitcast_fusion
  2.5 1.4 reshape.29.vec
  3.9 1.0 convert_element_type.62
  4.9 0.1 fusion.51
  5.0 0.6 copy.22
  5.7 0.6 copy.23
  7.0 88.4 %front.1 = (bf16[768,768]{1,0:T(8,128)(2,1)}, bf16[768,768]{1,0:T(8,128)(2,1)}, bf16[768,768]{1,0:T(8,128)(2,1)}, bf16[768,768]{1,0:T(8,128)(2,1)}, bf16[768,768...) custom-call(bf16[960,768]{1,0:T(8,128)(2,1)} %bitcast.35, ...), custom_call_target="tpu_custom_call" | custom-call | tf_op jit(solution)/shard_map/front/pallas_call | solution.py:530
  95.4 46.4 %mlp_back.1 = (bf16[960,768]{1,0:T(8,128)(2,1)}, f32[960,768]{1,0:T(8,128)}, bf16[960,384]{1,0:T(8,128)(2,1)}, bf16[768,1536]{1,0:T(8,128)(2,1)}, bf16[768,1920]{1,0:T(8,128)(2,1)}, /*index=5*/f32[8,768]{1,0:T(8,128)}) custom-call(bf16[960,768]{1,0:T(8,128)(2,1)} %bitcast.37, f32[12,768]{1,0:T(8,128)} %reshape.29.vec, ...), custom_call_target="tpu_custom_call" | custom-call | tf_op jit(solution)/shard_map/mlp_back/pallas_call | solution.py:684
  141.8 0.6 broadcast_in_dim.20.included
  142.4 109.5 %attn_back.1 = (bf16[960,768]{1,0:T(8,128)(2,1)}, f32[48,4,384]{2,1,0:T(4,128)}, f32[48,2,1536]{2,1,0:T(2,128)}, f32[12,768]{1,0:T(8,128)}, bf16[768,1536]{1,0:T(8,128)(2,1)}) custom-call(bf16[960,768]{1,0:T(8,128)(2,1)} %bitcast.36, f32[12,768]{1,0:T(8,128)} %reshape.29.vec, bf16[960,768]{1,0:T(8,128)(2,1)} %get-tuple-element.48.first, ...), custom_call_target="tpu_custom_call" | custom-call | tf_op jit(solution)/shard_map/attn_back/pallas_call | solution.py:1076
  251.9 0.0 copy-start.8
  252.0 0.0 copy-start.7
  252.0 0.0 copy-start.9
  252.0 0.0 copy-start.10
  252.0 4.4 %fusion.52 = f32[768,768]{1,0:T(8,128)S(1)} fusion(bf16[768,1536]{1,0:T(8,128)(2,1)} %get-tuple-element.62), kind=kOutput, calls=%fused_computation.75 | convolution fusion | flops 1811939328 | bytes 4718592 | tf_op jit(solution)/shard_map/dot_general | solution.py:44
  256.4 0.0 copy-start.2
  256.4 0.1 collective-permute-start
  256.5 0.0 copy-done.8
  256.5 0.0 copy-done.7
  256.5 0.0 copy-done.9
  256.6 0.0 copy-done.10
  256.6 0.8 multiply_subtract_fusion
  257.4 0.5 copy-done.2
  257.9 3.3 collective-permute-done
  261.2 3.3 select_reduce_fusion
  265.2 1.1 multiply_add_fusion.15
  266.3 1.1 fusion.30
  267.4 1.2 multiply_add_fusion.12
  268.6 1.1 add_convert_fusion.1
  269.7 1.1 multiply_add_fusion.10
  270.9 1.1 multiply_add_fusion.14
  272.0 1.1 multiply_add_fusion.9
  273.1 1.1 add_convert_fusion
  274.2 1.1 multiply_add_fusion.7
  275.3 1.1 multiply_add_fusion.6
  276.4 3.2 fusion.53
  279.6 3.2 multiply_add_fusion.1
  282.8 3.2 multiply_add_fusion
  286.0 3.0 fusion.54
  289.0 1.3 multiply_add_fusion.11
  290.4 3.2 multiply_add_fusion.8
  293.6 0.0 copy-start.11
  293.6 3.2 multiply_convert_fusion
  296.8 0.0 copy-done.11
  296.8 0.0 copy-start
  296.8 0.0 copy-start.1
  296.8 2.0 convolution_convert_fusion.orth
  298.8 0.0 copy-done
  298.8 0.0 copy-done.1
  298.8 0.0 copy-start.3
  298.9 0.0 copy-start.4
  298.9 44.1 %scatter_rows.1 = (f32[48,4,384]{2,1,0:T(4,128)S(1)}, f32[48,2,1536]{2,1,0:T(2,128)S(1)}) custom-call(bf16[768,1536]{1,0:T(8,128)(2,1)S(1)} %convolution_convert_fusion.orth, f32[48,4,384]{2,1,0:T(4,128)S(1)} %copy-done.1, f32[48,2,1536]{2,1,0:T(2,128)S(1)} %copy-done), custom_call_target="tpu_custom_call" | custom-call | tf_op jit(solution)/shard_map/scatter_rows/pallas_call | solution.py:148
  343.0 0.0 copy-done.3
  343.0 0.0 copy-start.6
  343.0 1.1 copy.33
  344.1 0.0 copy-done.4
  344.1 1.1 copy.34
  345.2 0.0 copy-done.6
  345.2 0.7 copy.35
  345.9 0.0 copy-done.5
  345.9 0.8 copy.36
  346.8 0.7 copy.37
  347.5 0.8 copy.38
  (2 shorter events, 0.0 us)
Async XLA Ops:
  251.9 4.6 %copy-start.8 = (f32[12,768]{1,0:T(8,128)S(1)}, f32[12,768]{1,0:T(8,128)}, u32[]{:S(2)}) copy-start(f32[12,768]{1,0:T(8,128)} %get-tuple-element.65) | copy-start | bytes 110596
  252.0 4.6 %copy-start.7 = (f32[9216]{0:T(1024)S(1)}, f32[9216]{0:T(1024)}, u32[]{:S(2)}) copy-start(f32[9216]{0:T(1024)} %param.21) | copy-start | bytes 110596
  252.0 4.6 %copy-start.9 = (f32[9216]{0:T(1024)S(1)}, f32[9216]{0:T(1024)}, u32[]{:S(2)}) copy-start(f32[9216]{0:T(1024)} %param.23) | copy-start | bytes 110596
  252.0 4.6 %copy-start.10 = (f32[9216]{0:T(1024)S(1)}, f32[9216]{0:T(1024)}, u32[]{:S(2)}) copy-start(f32[9216]{0:T(1024)} %param.22) | copy-start | bytes 110596
  256.4 1.4 copy-start.2
  256.4 4.7 %collective-permute-start = (f32[768,768]{1,0:T(8,128)S(1)}, f32[768,768]{1,0:T(8,128)}, u32[]{:S(2)}, u32[]{:S(2)}) collective-permute-start(f32[768,768]{1,0:T(8,128)S(1)} %fusion.52), channel_id=1, source_target_pairs={{0,1},{1,0},{2,3},{3,2},{4,5},{5,4},{6,7},{7,6},{8,9},{9,8},{10,11... | collective-permute-start | bytes 7077896 | tf_op jit(solution)/shard_map/ppermute | solution.py:1130
  293.6 3.3 copy-start.11
  296.8 2.0 copy-start
  296.8 2.0 copy-start.1
  298.8 44.1 %copy-start.3 = (bf16[960,768]{1,0:T(8,128)(2,1)S(1)}, bf16[960,768]{1,0:T(8,128)(2,1)}, u32[]{:S(2)}) copy-start(bf16[960,768]{1,0:T(8,128)(2,1)} %get-tuple-element.47) | copy-start | bytes 4423684
  298.9 45.3 %copy-start.4 = (bf16[960,768]{1,0:T(8,128)(2,1)S(1)}, bf16[960,768]{1,0:T(8,128)(2,1)}, u32[]{:S(2)}) copy-start(bf16[960,768]{1,0:T(8,128)(2,1)} %get-tuple-element.59) | copy-start | bytes 4423684
  343.0 2.2 copy-start.6
  344.1 1.8 copy-start.5
